TPU v7x, 256 devices: a whole 4x4x8 slice. The times are simulated.
256 devices in a mesh: query: 8 (over x_hi, y), ref: 32 (over x_lo, z, core).
Axes of the slice: x: 4 (x_hi: 2, x_lo: 2; x = x_hi * 2 + x_lo), y: 4, z: 8, core: 2. Of those that a mesh axis runs over, the one named last changes fastest.
Arguments:
- noise_field: bfloat16 [2048, 12288], P('query'), may hold values from -6 to 6
- ref_crops: bfloat16 [9216, 12288], P('ref'), may hold values from -3 to 3
- level_index: int32 [2048], P('query'), may hold values from 0 to 31
- query_ids: int32 [2048], P('query'), may hold values from 0 to 9215
- w_in: bfloat16 [192, 768], replicated, may hold values from -0.4375 to 0.4375
- bias_hidden: float32 [768], replicated, may hold values from -3 to 3
- w_noise: float32 [768], replicated, may hold values from -4 to 4
- w_out: bfloat16 [768, 192], replicated, may hold values from -0.21875 to 0.21875
Outputs:
- grad_w_in: float32 [192, 768], replicated
- grad_w_out: float32 [768, 192], replicated
- grad_bias: float32 [768], replicated
- grad_noise: float32 [768], replicated
- loss: float32 [], replicated
All inputs are finite; a program needn't handle non-finite values.
Results may differ from a plain program's by a relative error of at most 0.0013.
Values may be sent and summed in bfloat16 or wider, within the bound.
A program may use at most 128 MiB of HBM per device.

v0:
```python
import jax
import jax.numpy as jnp
from jax import lax
from jax.sharding import PartitionSpec as P

NLEV = 32


sigma_data = 0.5


def noise_level(index):
    low = 0.05 ** (1.0 / 7.0)
    high = 80.0 ** (1.0 / 7.0)
    frac = index.astype(jnp.float32) / (NLEV - 1)
    return (high + frac * (low - high)) ** 7


def tdot(left, right):
    return lax.dot_general(
        left, right, (((0,), (0,)), ((), ())), preferred_element_type=jnp.float32
    )


def forward_rows(x_rows, target_rows, sig_rows, w_in, bias_hidden, w_noise, w_out, queries):
    var = sig_rows * sig_rows + sigma_data * sigma_data
    c_skip = sigma_data * sigma_data / var
    c_out = sig_rows * sigma_data / jnp.sqrt(var)
    c_in = 1.0 / jnp.sqrt(var)
    c_noise = jnp.log(sig_rows) / 4.0
    x_full = x_rows.astype(jnp.float32)
    scaled = (c_in[:, None] * x_full).astype(jnp.bfloat16)
    pre = (
        jnp.dot(scaled, w_in, preferred_element_type=jnp.float32)
        + c_noise[:, None] * w_noise[None, :]
        + bias_hidden[None, :]
    )
    hidden = jax.nn.silu(pre).astype(jnp.bfloat16)
    output = jnp.dot(hidden, w_out, preferred_element_type=jnp.float32)
    resid = output - (target_rows - c_skip[:, None] * x_full) / c_out[:, None]
    objective = jnp.sum(resid * resid) / queries
    g_b = (2.0 / queries * resid).astype(jnp.bfloat16)
    g_out = tdot(hidden, g_b)
    return (scaled, pre, c_noise, g_b, g_out, objective)


def backward_rows(scaled, pre, c_noise, g_b, w_out):
    back = lax.dot_general(g_b, w_out, (((1,), (1,)), ((), ())), preferred_element_type=jnp.float32)
    sig_p = jax.nn.sigmoid(pre)
    dpre = back * sig_p * (1.0 + pre * (1.0 - sig_p))
    g_in = tdot(scaled, dpre.astype(jnp.bfloat16))
    return (g_in, jnp.sum(dpre, axis=0), jnp.sum(c_noise[:, None] * dpre, axis=0))


def per_device(noise_field, ref_crops, level_index, query_ids, w_in, bias_hidden, w_noise, w_out):
    ref_count = lax.axis_size("ref")
    rank = lax.axis_index("ref")
    ref_dev = ref_crops.shape[0]
    q_dev = noise_field.shape[0]
    feats = noise_field.shape[1]
    pdim = w_in.shape[0]
    queries = q_dev * lax.axis_size("query")
    local_ids = query_ids - rank * ref_dev
    inside = (local_ids >= 0) & (local_ids < ref_dev)
    picked_rows = jnp.take(ref_crops, jnp.clip(local_ids, 0, ref_dev - 1), axis=0)
    picked = jnp.where(inside[:, None], picked_rows.astype(jnp.float32), 0.0)
    clean = lax.psum(picked.astype(jnp.bfloat16), "ref")
    sigma = noise_level(level_index)
    noisy = (clean.astype(jnp.float32) + sigma[:, None] * noise_field.astype(jnp.float32)).astype(
        jnp.bfloat16
    )
    ref_sq = jnp.sum(jnp.square(ref_crops.astype(jnp.float32)), axis=1)
    dots = lax.dot_general(
        noisy, ref_crops, (((1,), (1,)), ((), ())), preferred_element_type=jnp.float32
    )
    score = (2.0 * dots - ref_sq[None, :]) / (2.0 * sigma[:, None] * sigma[:, None])
    peak = lax.pmax(jnp.max(score, axis=1), "ref")
    weights = jnp.exp(score - peak[:, None]).astype(jnp.bfloat16)
    total_part = jnp.sum(weights.astype(jnp.float32), axis=1)
    acc = jnp.dot(weights, ref_crops, preferred_element_type=jnp.float32)
    share = lax.psum_scatter(
        acc.astype(jnp.bfloat16), "ref", scatter_dimension=1, tiled=True
    ).astype(jnp.float32)
    total = lax.psum(total_part, "ref")
    width = feats // ref_count
    x_part = lax.dynamic_slice_in_dim(noisy, rank * width, width, 1)
    target = share / total[:, None]
    x_rows = x_part.reshape(-1, pdim)
    target_rows = target.reshape(-1, pdim)
    sig_rows = jnp.repeat(sigma, width // pdim)
    scaled, pre, c_noise, g_b, g_out, objective = forward_rows(
        x_rows, target_rows, sig_rows, w_in, bias_hidden, w_noise, w_out, queries
    )
    g_in, g_bias, g_noise = backward_rows(scaled, pre, c_noise, g_b, w_out)
    g_in_all, g_out_all, g_bias_all, g_noise_all, objective_all = lax.psum(
        (g_in, g_out, g_bias, g_noise, objective), ("query", "ref")
    )
    return (g_in_all, g_out_all, g_bias_all, g_noise_all, objective_all / feats)


def solution(mesh):
    return jax.shard_map(
        per_device,
        mesh=mesh,
        in_specs=(P("query", None), P("ref", None), P("query"), P("query"), P(), P(), P(), P()),
        out_specs=(P(), P(), P(), P(), P()),
        check_vma=False,
    )
```

profile of v0, /device:TPU:1, one launch (start us, length us, event | category | flops | bytes accessed | tf_op | source)
XLA Modules:
  0.0 762.3 jit_solution(5755416346121059087)
XLA Ops:
  7.2 0.0 copy-start
  7.2 0.0 all-reduce.5.cloned.1.call-start
  7.2 0.7 compare_and_fusion
  8.0 16.7 %gather_fusion = bf16[256,12288]{1,0:T(8,128)(2,1)} fusion(bf16[288,12288]{1,0:T(8,128)(2,1)} %param.9, s32[1024]{0:T(1024)S(1)} %pad_clamp_fusion), kind=kCustom, calls=%fused_computation | custom fusion | bytes 12583936 | tf_op jit(solution)/shard_map/jit(_take)/gather | solution.py:65
  24.6 9.0 %select_convert_fusion = bf16[256,12288]{1,0:T(8,128)(2,1)} fusion(bf16[256,12288]{1,0:T(8,128)(2,1)} %gather_fusion, pred[256]{0:T(512)(128)(4,1)S(1)} %get-tuple-element.14, pred[256]{0:T(512)(128)(4,1)S(1)} %get-tuple-element.20), kind=kLoop, calls=%fused_computation.4 | loop fusion | flops 12582912 | bytes 12583424 | tf_op jit(solution)/shard_map/convert_element_type | solution.py:67
  33.7 0.0 copy-start.3
  33.7 0.0 all-reduce.5.cloned.1.call-update
  33.7 0.0 reduce-scatter.4.cloned.1.call-start
  33.8 0.6 copy-done.3
  34.4 4.5 multiply_reduce_fusion
  38.9 239.7 %all-reduce.5.cloned.1.call-done = bf16[256,12288]{1,0:T(8,128)(2,1)} async-done(((bf16[256,12288]{1,0:T(8,128)(2,1)}), bf16[256,12288]{1,0:T(8,128)(2,1)}) %all-reduce.5.cloned.1.call-update) | async-done | bytes 6291472 | tf_op jit(solution)/shard_map/psum | solution.py:67
  278.5 7.2 add_convert_fusion
  285.8 0.0 copy-start.1
  285.8 8.0 %fusion.11 = (f32[256]{0:T(256)S(1)}, f32[256,288]{0,1:T(8,128)}) fusion(f32[256]{0:T(256)S(1)} %get-tuple-element.17, f32[288]{0:T(512)S(1)} %multiply_reduce_fusion, bf16[256,12288]{1,0:T(8,128)(2,1)S(1)} %add_convert_fusion, bf16[288,12288]{1,0:T(8,128)(2,1)} %param.9), kind=kOutput, calls=%fused_computation.39 | convolution fusion | flops 1812233984 | bytes 13667456 | tf_op jit(solution)/shard_map/dot_general | solution.py:73
  293.8 0.0 copy-done.1
  293.8 53.4 %pmax.7 = f32[256]{0:T(256)S(1)} all-reduce(f32[256]{0:T(256)S(1)} %get-tuple-element.23), channel_id=1, replica_groups=mesh['query'=8,'ref'=32] {'ref'}, use_global_device_ids=true, to_apply=%region_3.4 | all-reduce | flops 256 | bytes 2048 | tf_op jit(solution)/shard_map/pmax | solution.py:77
  347.2 9.2 %convolution_convert_fusion = bf16[256,12288]{1,0:T(8,128)(2,1)} fusion(bf16[288,12288]{1,0:T(8,128)(2,1)} %param.9, f32[256,288]{0,1:T(8,128)} %get-tuple-element.24, f32[256]{0:T(256)S(1)} %pmax.7), kind=kOutput, calls=%fused_computation.1 | convolution fusion | flops 1815232512 | bytes 13665280 | tf_op jit(solution)/shard_map/dot_general | solution.py:80
  356.4 8.6 %copy.17 = bf16[256,12288]{0,1:T(8,128)(2,1)} copy(bf16[256,12288]{1,0:T(8,128)(2,1)} %convolution_convert_fusion) | data formatting | bytes 12582912
  365.0 0.0 copy-start.2
  365.0 0.0 copy-start.5
  365.0 0.0 copy-start.6
  365.0 0.0 reduce-scatter.4.cloned.1.call-update
  365.1 0.0 all-reduce.7.cloned.1.call-start
  365.1 0.1 broadcast_in_dim.53
  365.2 0.1 div.62
  365.4 0.1 broadcast_in_dim.47
  365.5 0.1 sqrt.9
  365.6 0.1 broadcast_in_dim.55
  365.7 0.1 mul.161
  365.9 0.1 broadcast_in_dim.54
  366.0 0.1 div.69
  366.1 1.0 dynamic-slice_convert_fusion
  367.1 0.1 reshape.69
  367.2 0.0 copy-start.4
  367.2 0.2 copy.15
  367.4 0.0 copy-done.2
  367.4 0.1 convert_reduce_fusion
  367.5 56.8 %psum.50 = f32[256]{0:T(256)S(1)} all-reduce(f32[256]{0:T(256)S(1)} %convert_reduce_fusion), channel_id=1, replica_groups=mesh['query'=8,'ref'=32] {'ref'}, use_global_device_ids=true, to_apply=%region_6.7 | all-reduce | flops 256 | bytes 2048 | tf_op jit(solution)/shard_map/psum | solution.py:84
  424.3 0.0 copy-done
  424.3 0.0 copy-done.5
  424.3 0.0 copy-done.6
  424.3 1.8 multiply_convert_fusion
  426.1 60.6 %reduce-scatter.4.cloned.1.call-done = bf16[384,256]{1,0:T(8,128)(2,1)} async-done(((bf16[12288,256]{1,0:T(8,128)(2,1)}), bf16[384,256]{1,0:T(8,128)(2,1)}) %reduce-scatter.4.cloned.1.call-update) | async-done | bytes 196624
  486.7 1.1 copy.18
  487.8 0.1 convert_divide_fusion
  487.9 0.1 reshape.68
  488.1 0.2 copy.16
  488.2 0.0 copy-done.4
  488.3 1.1 multiply_reduce_fusion.2
  489.3 1.1 fusion.4
  490.5 2.3 multiply_reduce_fusion.1
  492.8 1.3 fusion.2
  494.1 0.0 all-reduce.7.cloned.1.call-update
  494.7 78.6 %all-reduce = (f32[768]{0:T(1024)}, f32[768]{0:T(1024)}, f32[]{:T(128)}) all-reduce(f32[768]{0:T(1024)S(1)} %get-tuple-element.6, f32[768]{0:T(1024)S(1)} %get-tuple-element.5, f32[]{:T(128)S(6)} %div.73), channel_id=1, replica_groups=mesh['query'=8,'ref'=32] {'query','ref'}, use_global_device_ids=true, to_apply=%region_10.11 | all-reduce | flops 1537 | bytes 12296 | tf_op jit(solution)/shard_map/psum | solution.py:95
  574.0 176.8 %all-reduce.7.cloned.1.call-done = (f32[192,768]{1,0:T(8,128)}, f32[768,192]{0,1:T(8,128)}) async-done(((f32[192,768]{1,0:T(8,128)}, f32[768,192]{0,1:T(8,128)}), (f32[192,768]{1,0:T(8,128)}, f32[768,192]{0,1:T(8,128)})) %all-reduce.7.cloned.1.call-update) | async-done | bytes 1179664 | tf_op jit(solution)/shard_map/psum | solution.py:95
  750.8 1.9 copy.22
  752.8 1.9 copy.23
  (4 shorter events, 0.0 us)
Async XLA Ops:
  7.2 417.2 %copy-start = (bf16[192,768]{1,0:T(8,128)(2,1)S(1)}, bf16[192,768]{1,0:T(8,128)(2,1)}, u32[]{:S(2)}) copy-start(bf16[192,768]{1,0:T(8,128)(2,1)} %param.12) | copy-start | bytes 884740
  7.2 271.4 %all-reduce.5.cloned.1.call-start = ((), (), s32[]{:S(2)}) async-start(), calls=%async_computation.1 | async-start | bytes 12582912 | tf_op jit(solution)/shard_map/psum | solution.py:67
  33.7 0.7 copy-start.3
  33.7 453.0 %reduce-scatter.4.cloned.1.call-start = ((), (), s32[]{:S(2)}) async-start(), calls=%async_computation.2 | async-start | bytes 6488064
  285.8 8.0 %copy-start.1 = (bf16[256,12288]{1,0:T(8,128)(2,1)}, bf16[256,12288]{1,0:T(8,128)(2,1)S(1)}, u32[]{:S(2)}) copy-start(bf16[256,12288]{1,0:T(8,128)(2,1)S(1)} %add_convert_fusion) | copy-start | bytes 18874372
  365.0 2.4 copy-start.2
  365.0 59.3 %copy-start.5 = (f32[768]{0:T(1024)S(1)}, f32[768]{0:T(1024)}, u32[]{:S(2)}) copy-start(f32[768]{0:T(1024)} %param.13) | copy-start | bytes 9220
  365.0 59.3 %copy-start.6 = (f32[768]{0:T(1024)S(1)}, f32[768]{0:T(1024)}, u32[]{:S(2)}) copy-start(f32[768]{0:T(1024)} %param.14) | copy-start | bytes 9220
  365.1 385.8 %all-reduce.7.cloned.1.call-start = ((), (), s32[]{:S(2)}) async-start(), calls=%async_computation.3 | async-start | bytes 2359296 | tf_op jit(solution)/shard_map/psum | solution.py:95
  367.2 121.0 %copy-start.4 = (bf16[768,192]{0,1:T(8,128)(2,1)S(1)}, bf16[768,192]{0,1:T(8,128)(2,1)}, u32[]{:S(2)}) copy-start(bf16[768,192]{0,1:T(8,128)(2,1)} %param.15) | copy-start | bytes 884740
Sparse Core Ops, SparseCore 0:
  33.8 244.6 all-reduce.4
  365.2 121.4 reduce-scatter.3
  494.2 256.5 all-reduce.6
where the time goes:
time: 765 us; the launch traced here: 762 us
  waiting for transfers between devices  477 us (62%)
  blocking collectives  189 us (25%)
  local copies, waits for them, and re-layouts  32.4 us (4%)
  matrix products  24.8 us (3%)
  other arithmetic  22.7 us (3%)
  between operations  16.3 us (2%)
    psum x1, waiting for transfers between devices, per_device(): clean = lax.psum(picked.astype(jnp.bfloat16), 'ref')  240 us
    psum x1, waiting for transfers between devices, per_device(): lax.psum((g_in, g_out, g_bias, g_noise, objective), ('query', 'ref'))  177 us
    psum x1, blocking collectives, per_device(): lax.psum((g_in, g_out, g_bias, g_noise, objective), ('query', 'ref'))  78.6 us
    unnamed x4, waiting for transfers between devices  60.6 us
    psum x1, blocking collectives, per_device(): total = lax.psum(total_part, 'ref')  56.8 us
    pmax x1, blocking collectives, per_device(): peak = lax.pmax(jnp.max(score, axis=1), 'ref')  53.4 us
    gather x1, local copies, waits for them, and re-layouts, per_device(): jnp.take(ref_crops, jnp.clip(local_ids, 0, ref_dev - 1), axis=0)  16.7 us
  transfers between devices with their start and end apart: 3, of which 3 were waited for; matrix products, arithmetic and copies ran while one was open for 1% of the time, Pallas kernels for 0%

commit v1 on v0

v1 whole, which is shorter than its diff:
```python
import jax
import jax.numpy as jnp
from jax import lax
from jax.experimental import pallas as pl
from jax.experimental.pallas import tpu as pltpu
from jax.sharding import PartitionSpec as P

NLEV = 32
SIGMA_DATA = 0.5
MESH = pl.DeviceIdType.MESH
F32 = jnp.float32
BF16 = jnp.bfloat16

Z = 8
CHIPS = 2 * Z
Q = 256
HALF = 128
REF = 288
PAIR = 2 * REF
W = 384
PDIM = 192
HID = 768
NQ = 2048
FEATS = 12288


def nt(a, b, **kw):
    return lax.dot_general(a, b, (((1,), (1,)), ((), ())), preferred_element_type=F32, **kw)


def tn(a, b, **kw):
    return lax.dot_general(a, b, (((0,), (0,)), ((), ())), preferred_element_type=F32, **kw)


def nn(a, b):
    return jnp.dot(a, b, preferred_element_type=F32)


def noise_level(index):
    low = 0.05 ** (1.0 / 7.0)
    high = 80.0 ** (1.0 / 7.0)
    frac = index.astype(F32) / (NLEV - 1)
    base = high + frac * (low - high)
    two = base * base
    return two * two * two * base


def column(row):
    return jnp.broadcast_to(row, (128, row.shape[1])).T[:, 0:1]


def row_of(col):
    return jnp.broadcast_to(col, (col.shape[0], 128)).T[0:8]


def main_kernel(
    noise_hbm, refs_hbm, level_ref, ids_ref, w_in_ref, bias_ref, w_noise_ref, w_outT_ref,
    grad_ref,
    refs, prod, match, noisy, noise, dots, halfS, halfR, statS, statR, sqacc,
    axS, axR, azS, azR, bzS, bzR, bxS, bxR, shareS,
    local_sem, swap_ss, swap_rs, half_sem, stat_ss, stat_rs,
    ax_ss, ax_rs, az_ss, az_rs, bz_ss, bz_rs, bx_ss, bx_rs,
    gax_ss, gax_rs, gaz_ss, gaz_rs, gbz_ss, gbz_rs, gbx_ss, gbx_rs,
):
    q = lax.axis_index("query")
    r = lax.axis_index("ref")
    core = r % 2
    chip = r // 2
    z = chip % Z
    xl = chip // Z
    other = 1 - xl

    def at(x_at, z_at, core_at):
        return (x_at * Z + z_at) * 2 + core_at

    sib = at(xl, z, 1 - core)
    xn = at(other, z, core)
    to = (at(xl, (z + Z - 1) % Z, core), at(xl, (z + 1) % Z, core))

    def rcopy(src, dst, ssem, rsem, target):
        return pltpu.make_async_remote_copy(
            src_ref=src, dst_ref=dst, send_sem=ssem, recv_sem=rsem,
            device_id=(q, target), device_id_type=MESH)

    def order(i):
        d = 4 - (i + 1) // 2
        return (z + Z + d * (2 * (i % 2) - 1)) % Z

    def local_copy(b):
        off = pl.multiple_of(core * (FEATS // 2) + b * W, 128)
        return pltpu.make_async_copy(
            refs_hbm.at[:, pl.ds(off, W)], refs.at[b, pl.ds(core * REF, REF), :], local_sem.at[b])

    def swap_copy(b):
        off = pl.multiple_of((1 - core) * (FEATS // 2) + b * W, 128)
        return rcopy(
            refs_hbm.at[:, pl.ds(off, W)], refs.at[b, pl.ds(core * REF, REF), :],
            swap_ss.at[b], swap_rs.at[b], sib)

    def swap_landed(b):
        return rcopy(
            refs_hbm.at[:, pl.ds(0, W)], refs.at[b, pl.ds((1 - core) * REF, REF), :],
            swap_ss.at[b], swap_rs.at[b], sib)

    own = 2 * z + xl

    def start_local(i, _):
        o = order(i)
        local_copy(2 * o).start()
        local_copy(2 * o + 1).start()
        return 0

    lax.fori_loop(0, Z, start_local, 0)
    noise_off = pl.multiple_of(core * (FEATS // 2) + own * W, 128)
    noise_copy = pltpu.make_async_copy(
        noise_hbm.at[:, pl.ds(noise_off, W)], noise, local_sem.at[2 * Z])
    noise_copy.start()

    barrier = pltpu.get_barrier_semaphore()

    def greet(k, _):
        peer = (chip + k) % CHIPS
        pl.semaphore_signal(barrier, inc=1, device_id=(q, peer * 2 + core), device_id_type=MESH)
        return 0

    lax.fori_loop(1, CHIPS, greet, 0)
    pl.semaphore_signal(barrier, inc=1, device_id=(q, sib), device_id_type=MESH)
    pl.semaphore_wait(barrier, CHIPS)

    def start_swap(i, _):
        o = order(i)
        swap_copy(2 * o).start()
        swap_copy(2 * o + 1).start()
        return 0

    lax.fori_loop(0, Z, start_swap, 0)

    sigma = noise_level(level_ref[...])
    sigma_col = column(sigma)
    ids = column(ids_ref[...].astype(F32)) - (chip * PAIR).astype(F32)
    places = lax.broadcasted_iota(jnp.int32, (Q, PAIR), 1).astype(F32)
    match[...] = (ids == places).astype(F32).astype(BF16)

    def reduce_scatter(ph):
        def ax(o):
            return rcopy(axS.at[ph, o], axR.at[ph, o], ax_ss.at[ph, o], ax_rs.at[ph, o], xn)

        def az(d, t):
            if t == 0:
                rows = pl.ds(64 * d, 64)
                return rcopy(azS.at[ph, d, 0, rows], azR.at[ph, d, 0, rows],
                             az_ss.at[ph, d, 0], az_rs.at[ph, d, 0], to[d])
            return rcopy(azS.at[ph, d, t], azR.at[ph, d, t],
                         az_ss.at[ph, d, t], az_rs.at[ph, d, t], to[d])

        def bz(d, t):
            if t == 0:
                return rcopy(bzS.at[ph, d, 0, d], bzR.at[ph, d, 0, d],
                             bz_ss.at[ph, d, 0], bz_rs.at[ph, d, 0], to[d])
            return rcopy(bzS.at[ph, d, t], bzR.at[ph, d, t],
                         bz_ss.at[ph, d, t], bz_rs.at[ph, d, t], to[d])

        def bx():
            return rcopy(bxS.at[ph], bxR.at[ph], bx_ss.at[ph], bx_rs.at[ph], xn)

        def multiply(i, _):
            o = order(i)
            for j in range(2):
                b = 2 * o + j
                if ph == 0:
                    local_copy(b).wait()
                    swap_landed(b).wait_recv()
                prod[b] = nn(match[...], refs[b])
            axS[ph, o] = prod[2 * o + other, 0:HALF].astype(BF16)
            ax(o).start()
            return 0

        multiply(0, 0)
        o = order(0)
        for d in range(2):
            bzS[ph, d, 0, d] = prod[2 * o + d, HALF:Q].astype(BF16)
            bz(d, 0).start()
        lax.fori_loop(1, Z, multiply, 0)

        ax(o).wait_recv()
        for d in range(2):
            rows = slice(64 * d, 64 * d + 64)
            azS[ph, d, 0, rows] = (prod[2 * o + xl, rows] + axR[ph, o, rows].astype(F32)).astype(BF16)
            az(d, 0).start()
        for t in range(1, 4):
            for d in range(2):
                o = (z + Z + (2 * d - 1) * (4 - t)) % Z
                bz(d, t - 1).wait_recv()
                for j in range(2):
                    s = prod[2 * o + j, HALF:Q]
                    if t > 1 or j == d:
                        s = s + bzR[ph, d, t - 1, j].astype(F32)
                    bzS[ph, d, t, j] = s.astype(BF16)
                bz(d, t).start()
            for d in range(2):
                o = (z + Z + (2 * d - 1) * (4 - t)) % Z
                ax(o).wait_recv()
                az(d, t - 1).wait_recv()
                s = prod[2 * o + xl, 0:HALF] + axR[ph, o].astype(F32)
                if t > 1:
                    azS[ph, d, t] = (s + azR[ph, d, t - 1].astype(F32)).astype(BF16)
                else:
                    azS[ph, d, t] = s.astype(BF16)
                    rows = slice(64 * d, 64 * d + 64)
                    azS[ph, d, t, rows] = (s[rows] + azR[ph, d, 0, rows].astype(F32)).astype(BF16)
                az(d, t).start()
        for d in range(2):
            bz(d, 3).wait_recv()
        bxS[ph] = (prod[2 * z + other, HALF:Q] + bzR[ph, 0, 3, other].astype(F32)
                   + bzR[ph, 1, 3, other].astype(F32)).astype(BF16)
        bx().start()
        ax(z).wait_recv()
        for d in range(2):
            az(d, 3).wait_recv()
        top = (prod[own, 0:HALF] + axR[ph, z].astype(F32)
               + azR[ph, 0, 3].astype(F32) + azR[ph, 1, 3].astype(F32))
        bottom = (prod[own, HALF:Q] + bzR[ph, 0, 3, xl].astype(F32)
                  + bzR[ph, 1, 3, xl].astype(F32))
        bx().wait_recv()
        bottom = bottom + bxR[ph].astype(F32)

        def finish():
            for d in range(2):
                for t in range(4):
                    az(d, t).wait_send()
                    bz(d, t).wait_send()
            bx().wait_send()

            def one(o, _):
                ax(o).wait_send()
                return 0

            lax.fori_loop(0, Z, one, 0)

        return top, bottom, finish

    top, bottom, finish0 = reduce_scatter(0)
    noise_copy.wait()
    noisy[own, 0:HALF] = (top + sigma_col[0:HALF] * noise[0:HALF].astype(F32)).astype(BF16)
    noisy[own, HALF:Q] = (bottom + sigma_col[HALF:Q] * noise[HALF:Q].astype(F32)).astype(BF16)

    def same(ref, ssem, rsem, target):
        return rcopy(ref, ref, ssem, rsem, target)

    def gax(o, x_at):
        return same(noisy.at[2 * o + x_at, 0:HALF], gax_ss.at[o], gax_rs.at[o], xn)

    def gbx(x_at):
        return same(noisy.at[2 * z + x_at, HALF:Q], gbx_ss.at[0], gbx_rs.at[0], xn)

    def gaz(d, s, o):
        if s == 4:
            view = noisy.at[2 * o + xl, pl.ds(64 * d, 64)]
        else:
            view = noisy.at[2 * o + xl, 0:HALF]
        return same(view, gaz_ss.at[d, s - 1], gaz_rs.at[d, s - 1], to[d])

    def gbz(d, s, o):
        if s == 4:
            view = noisy.at[2 * o + d, HALF:Q]
        else:
            view = noisy.at[pl.ds(2 * o, 2), HALF:Q]
        return same(view, gbz_ss.at[d, s - 1], gbz_rs.at[d, s - 1], to[d])

    def came(d, s):
        return (z + Z + (1 - 2 * d) * s) % Z

    def score(o, first=False):
        part = nt(noisy[2 * o], refs[2 * o]) + nt(noisy[2 * o + 1], refs[2 * o + 1])
        dots[...] = part if first else dots[...] + part

    gbx(xl).start()
    for d in range(2):
        gaz(d, 1, z).start()
    gax(z, xl).start()
    gbx(other).wait_recv()
    for d in range(2):
        gbz(d, 1, z).start()

    sqacc[...] = jnp.zeros_like(sqacc)

    def squares(b, _):
        v = refs[b].astype(F32)
        v = v * v
        sqacc[...] += v[:, 0:128] + v[:, 128:256] + v[:, 256:384]
        return 0

    lax.fori_loop(0, 2 * Z, squares, 0)

    for s in range(1, 4):
        for d in range(2):
            o = came(d, s)
            gaz(d, s, o).wait_recv()
            gaz(d, s + 1, o).start()
            gax(o, xl).start()
        for d in range(2):
            o = came(d, s)
            gbz(d, s, o).wait_recv()
            gbz(d, s + 1, o).start()
        if s == 1:
            gax(z, other).wait_recv()
            score(z, True)
        else:
            for d in range(2):
                o = came(d, s - 1)
                gax(o, other).wait_recv()
                score(o)
    o = came(0, 4)
    for d in range(2):
        gaz(d, 4, o).wait_recv()
    gax(o, xl).start()
    for d in range(2):
        gax(came(d, 3), other).wait_recv()
        score(came(d, 3))
    for d in range(2):
        gbz(d, 4, o).wait_recv()
    gax(o, other).wait_recv()
    score(o)

    ref_sq = nt(jnp.ones((8, 128), F32), sqacc[...], precision=lax.Precision.HIGHEST)[0:1]
    halfS[...] = 2.0 * dots[...] - ref_sq
    half = rcopy(halfS, halfR, half_sem.at[0], half_sem.at[1], sib)
    half.start()
    half.wait_recv()
    logits = (halfS[...] + halfR[...]) / (2.0 * sigma_col * sigma_col)
    dots[...] = logits

    def stat(i, k):
        peer = ((chip + k) % CHIPS) * 2 + core
        return rcopy(statS.at[i], statR.at[i, k], stat_ss.at[i, k], stat_rs.at[i, k], peer)

    def tell(i, col):
        statS[i] = row_of(col)
        statR[i, 0] = statS[i]

        def one(k, _):
            stat(i, k).start()
            return 0

        lax.fori_loop(1, CHIPS, one, 0)

    def hear(i):
        def one(k, _):
            stat(i, k).wait_recv()
            return 0

        lax.fori_loop(1, CHIPS, one, 0)

    tell(0, jnp.max(logits, axis=1, keepdims=True))
    hear(0)
    peak = column(jnp.max(statR[0], axis=0)[0:1])
    weights = jnp.exp(dots[...] - peak).astype(BF16)
    match[...] = weights
    tell(1, jnp.sum(weights.astype(F32), axis=1, keepdims=True))

    top, bottom, finish1 = reduce_scatter(1)
    shareS[0:HALF] = top
    shareS[HALF:Q] = bottom
    hear(1)
    total = jnp.sum(statR[1], axis=0)[0:1]

    def patches(t):
        return jnp.concatenate([t[0:PDIM], t[PDIM:W]], axis=1)

    def twice(t):
        return jnp.concatenate([t, t], axis=1)

    target = patches(shareS[...].T / total)
    x_full = patches(noisy[own].astype(F32).T)
    s = twice(sigma)
    var = s * s + SIGMA_DATA * SIGMA_DATA
    c_skip = SIGMA_DATA * SIGMA_DATA / var
    c_out = s * SIGMA_DATA / jnp.sqrt(var)
    c_in = 1.0 / jnp.sqrt(var)
    c_noise = jnp.log(s) / 4.0
    scaled = (c_in * x_full).astype(BF16)
    pre = tn(w_in_ref[...], scaled) + column(w_noise_ref[...]) * c_noise + column(bias_ref[...])
    sig_p = jax.nn.sigmoid(pre)
    hidden = (pre * sig_p).astype(BF16)
    resid = nn(w_outT_ref[...], hidden) - (target - c_skip * x_full) / c_out
    objective = jnp.sum(resid * resid) / NQ
    g_b = (2.0 / NQ * resid).astype(BF16)
    g_out = nt(g_b, hidden)
    back = tn(w_outT_ref[...], g_b)
    dpre = back * sig_p * (1.0 + pre * (1.0 - sig_p))
    g_in = nt(scaled, dpre.astype(BF16))
    rows = lax.broadcasted_iota(jnp.int32, (8, 2 * Q), 0)
    pick = jnp.where(rows == 0, 1.0, jnp.where(rows == 1, c_noise, 0.0))
    small = nt(pick, dpre, precision=lax.Precision.HIGHEST)
    small = jnp.where(lax.broadcasted_iota(jnp.int32, (8, HID), 0) == 2, objective, small)
    grad_ref[0:PDIM] = g_in
    grad_ref[PDIM:2 * PDIM] = g_out
    grad_ref[2 * PDIM:2 * PDIM + 8] = small

    finish0()
    finish1()

    def swap_sent(b, _):
        swap_copy(b).wait_send()
        return 0

    lax.fori_loop(0, 2 * Z, swap_sent, 0)
    half.wait_send()

    def stat_sent(k, _):
        stat(0, k).wait_send()
        stat(1, k).wait_send()
        return 0

    lax.fori_loop(1, CHIPS, stat_sent, 0)
    gbx(xl).wait_send()

    def gax_sent(o, _):
        gax(o, xl).wait_send()
        return 0

    lax.fori_loop(0, Z, gax_sent, 0)
    for d in range(2):
        for s in range(1, 5):
            gaz(d, s, z).wait_send()
            gbz(d, s, z).wait_send()


def main_call(noise, refs, level, ids, w_in, bias, w_noise, w_outT):
    dma = pltpu.SemaphoreType.DMA
    vm = pltpu.VMEM
    any_spec = pl.BlockSpec(memory_space=pl.ANY)
    vmem_spec = pl.BlockSpec(memory_space=pltpu.VMEM)
    return pl.pallas_call(
        main_kernel,
        out_shape=jax.ShapeDtypeStruct((2 * PDIM + 8, HID), F32),
        in_specs=[any_spec] * 2 + [vmem_spec] * 6,
        out_specs=vmem_spec,
        scratch_shapes=[
            vm((2 * Z, PAIR, W), BF16),
            vm((2 * Z, Q, W), F32),
            vm((Q, PAIR), BF16),
            vm((2 * Z, Q, W), BF16),
            vm((Q, W), BF16),
            vm((Q, PAIR), F32),
            vm((Q, PAIR), F32),
            vm((Q, PAIR), F32),
            vm((2, 8, Q), F32),
            vm((2, CHIPS, 8, Q), F32),
            vm((PAIR, 128), F32),
            vm((2, Z, HALF, W), BF16),
            vm((2, Z, HALF, W), BF16),
            vm((2, 2, 4, HALF, W), BF16),
            vm((2, 2, 4, HALF, W), BF16),
            vm((2, 2, 4, 2, HALF, W), BF16),
            vm((2, 2, 4, 2, HALF, W), BF16),
            vm((2, HALF, W), BF16),
            vm((2, HALF, W), BF16),
            vm((Q, W), F32),
            dma((2 * Z + 1,)), dma((2 * Z,)), dma((2 * Z,)), dma((2,)),
            dma((2, CHIPS)), dma((2, CHIPS)),
            dma((2, Z)), dma((2, Z)), dma((2, 2, 4)), dma((2, 2, 4)),
            dma((2, 2, 4)), dma((2, 2, 4)), dma((2,)), dma((2,)),
            dma((Z,)), dma((Z,)), dma((2, 4)), dma((2, 4)),
            dma((2, 4)), dma((2, 4)), dma((1,)), dma((1,)),
        ],
        compiler_params=pltpu.CompilerParams(
            collective_id=0, has_side_effects=True, vmem_limit_bytes=56 * 1024 * 1024),
        name="denoise_step",
    )(noise, refs, level, ids, w_in, bias, w_noise, w_outT)


def per_device(noise_field, ref_crops, level_index, query_ids, w_in, bias_hidden, w_noise, w_out):
    grads = main_call(
        noise_field, ref_crops, level_index.reshape(1, Q), query_ids.reshape(1, Q), w_in,
        bias_hidden.reshape(1, HID), w_noise.reshape(1, HID), w_out.T)
    grads = lax.psum(grads, ("query", "ref"))
    g_in = grads[0:PDIM]
    g_out = grads[PDIM:2 * PDIM].T
    small = grads[2 * PDIM:]
    return (g_in, g_out, small[0], small[1], small[2, 0] / FEATS)


def solution(mesh):
    return jax.shard_map(
        per_device,
        mesh=mesh,
        in_specs=(P("query", None), P("ref", None), P("query"), P("query"), P(), P(), P(), P()),
        out_specs=(P(), P(), P(), P(), P()),
        check_vma=False,
    )
```

time: 765 us -> 399 us (0.52)
  waiting for transfers between devices: 477 us -> 258 us
  blocking collectives: 189 us -> 0 us
  Pallas kernels: 0 us -> 116 us
  local copies, waits for them, and re-layouts: 32.4 us -> 7.48 us
  matrix products: 24.8 us -> 0 us
  other arithmetic: 22.7 us -> 0 us
    psum x2 -> x1, waiting for transfers between devices: 417 us -> 258 us  [per_device(): grads = lax.psum(grads, ('query', 'ref'))]
    psum x2 -> x0, blocking collectives: 135 us -> none  [the longest x1 78.6 us: per_device(): lax.psum((g_in, g_out, g_bias, g_noise, objective), ('query', 'ref'))]
    pallas_call x0 -> x1, Pallas kernels: none -> 116 us  [main_call(): pl.pallas_call(main_kernel, out_shape=jax.ShapeDtypeStruct((2 * PDIM + 8,...]
    unnamed x4 -> x1, waiting for transfers between devices: 60.6 us -> 0.02 us
    pmax x1 -> x0, blocking collectives: 53.4 us -> none  [per_device(): peak = lax.pmax(jnp.max(score, axis=1), 'ref')]
    dot_general x7 -> x0, matrix products: 24.8 us -> none  [the longest x1 9.2 us: per_device(): acc = jnp.dot(weights, ref_crops, preferred_element_type=jnp.float32)]
    convert_element_type x3 -> x0, other arithmetic: 17.2 us -> none  [the longest x1 9.04 us: per_device(): clean = lax.psum(picked.astype(jnp.bfloat16), 'ref')]
    gather x1 -> x0, local copies, waits for them, and re-layouts: 16.7 us -> none  [per_device(): jnp.take(ref_crops, jnp.clip(local_ids, 0, ref_dev - 1), axis=0)]
  transfers between devices with their start and end apart: 3 -> 1, of which waited for: 3 -> 1; matrix products, arithmetic and copies ran while one was open for 1% -> 0% of each run, Pallas kernels for 0% -> 0%
where the time goes in v1:
time: 399 us; the launch traced here: 397 us
  waiting for transfers between devices  258 us (65%)
  Pallas kernels  116 us (29%)
  between operations  15.8 us (4%)
  local copies, waits for them, and re-layouts  7.48 us (2%)
    psum x1, waiting for transfers between devices, per_device(): grads = lax.psum(grads, ('query', 'ref'))  258 us
    pallas_call x1, Pallas kernels, main_call(): pl.pallas_call(main_kernel, out_shape=jax.ShapeDtypeStruct((2 * PDIM + 8,...  116 us
  transfers between devices with their start and end apart: 1, of which 1 were waited for; matrix products, arithmetic and copies ran while one was open for 0% of the time, Pallas kernels for 0%

profile of v1, /device:TPU:1, one launch (start us, length us, event | category | flops | bytes accessed | tf_op | source)
XLA Modules:
  0.0 397.3 jit_solution(7880560682296659382)
XLA Ops:
  7.2 0.0 all-reduce.2.cloned.1.call-start
  7.2 1.3 reshape.26.bias_ref
  8.5 1.3 reshape.27.w_noise_ref
  9.7 115.8 %denoise_step.1 = f32[392,768]{1,0:T(8,128)} custom-call(bf16[256,12288]{1,0:T(8,128)(2,1)} %noise_hbm.1, bf16[288,12288]{1,0:T(8,128)(2,1)} %refs_hbm.1, s32[1,256]{1,0:T(1,128)} %bitcast.7, s32[1,256]{1,0:T(1,128)} %bitcast.8, bf16[192,768]{1,0:T(8,128)(2,1)} %w_in_ref.1, f32[1,768]{1,0:T(1,128)} %reshape.26.bias_ref, f32[1,768]{1,0:T(1,128)} %reshape.27.w_noise_ref, ...), custom_call_target="tpu_custom_call" | custom-call | tf_op jit(solution)/shard_map/denoise_step/pallas_call | solution.py:434
  125.5 0.0 all-reduce.2.cloned.1.call-update
  125.5 258.2 %all-reduce.2.cloned.1.call-done = f32[392,768]{1,0:T(8,128)} async-done(((f32[392,768]{1,0:T(8,128)}), f32[392,768]{1,0:T(8,128)}) %all-reduce.2.cloned.1.call-update) | async-done | bytes 1204240 | tf_op jit(solution)/shard_map/psum | solution.py:477
  383.7 1.2 slice.28
  385.5 1.4 slice_reduce_fusion
  387.0 2.3 slice_bitcast_fusion
Async XLA Ops:
  7.2 376.5 %all-reduce.2.cloned.1.call-start = ((), (), s32[]{:S(2)}) async-start(), calls=%async_computation | async-start | bytes 2408448 | tf_op jit(solution)/shard_map/psum | solution.py:477
Sparse Core Ops, SparseCore 0:
  125.7 257.9 all-reduce.1

commit v2 on v1

--- a/solution.py
+++ b/solution.py
@@ -22,6 +22,10 @@
 HID = 768
 NQ = 2048
 FEATS = 12288
+PLANE = 16
+PIECE = 80
+OWN = 16
+OWNERS = PIECE // OWN
 
 
 def nt(a, b, **kw):
@@ -54,13 +58,15 @@
 
 
 def main_kernel(
-    noise_hbm, refs_hbm, level_ref, ids_ref, w_in_ref, bias_ref, w_noise_ref, w_outT_ref,
-    grad_ref,
+    noise_hbm, refs_hbm, level_ref, ids_ref, w_in_ref, vec_ref, w_outT_ref,
+    g_in_ref, g_outT_ref, small_ref,
+    grads, coreR, planeS, planeR, zR, whole,
     refs, prod, match, noisy, noise, dots, halfS, halfR, statS, statR, sqacc,
     axS, axR, azS, azR, bzS, bzR, bxS, bxR, shareS,
     local_sem, swap_ss, swap_rs, half_sem, stat_ss, stat_rs,
     ax_ss, ax_rs, az_ss, az_rs, bz_ss, bz_rs, bx_ss, bx_rs,
     gax_ss, gax_rs, gaz_ss, gaz_rs, gbz_ss, gbz_rs, gbx_ss, gbx_rs,
+    core_ss, core_rs, plane_ss, plane_rs, z_ss, z_rs, back_ss, back_rs, share_ss, share_rs, swap2_ss, swap2_rs,
 ):
     q = lax.axis_index("query")
     r = lax.axis_index("ref")
@@ -73,6 +79,13 @@
     def at(x_at, z_at, core_at):
         return (x_at * Z + z_at) * 2 + core_at
 
+    x_hi = q // 4
+    y = q % 4
+    me = (x_hi * 2 + xl) * 4 + y
+
+    def in_plane(p):
+        return ((p // 8) * 4 + p % 4, at((p // 4) % 2, z, core))
+
     sib = at(xl, z, 1 - core)
     xn = at(other, z, core)
     to = (at(xl, (z + Z - 1) % Z, core), at(xl, (z + 1) % Z, core))
@@ -125,7 +138,19 @@
 
     lax.fori_loop(1, CHIPS, greet, 0)
     pl.semaphore_signal(barrier, inc=1, device_id=(q, sib), device_id_type=MESH)
-    pl.semaphore_wait(barrier, CHIPS)
+
+    def greet_plane(k, _):
+        p = (me + k) % PLANE
+
+        @pl.when(p != x_peer)
+        def _():
+            pl.semaphore_signal(barrier, inc=1, device_id=in_plane(p), device_id_type=MESH)
+
+        return 0
+
+    x_peer = (x_hi * 2 + other) * 4 + y
+    lax.fori_loop(1, PLANE, greet_plane, 0)
+    pl.semaphore_wait(barrier, CHIPS + PLANE - 2)
 
     def start_swap(i, _):
         o = order(i)
@@ -379,7 +404,7 @@
     c_in = 1.0 / jnp.sqrt(var)
     c_noise = jnp.log(s) / 4.0
     scaled = (c_in * x_full).astype(BF16)
-    pre = tn(w_in_ref[...], scaled) + column(w_noise_ref[...]) * c_noise + column(bias_ref[...])
+    pre = tn(w_in_ref[...], scaled) + column(vec_ref[1:2]) * c_noise + column(vec_ref[0:1])
     sig_p = jax.nn.sigmoid(pre)
     hidden = (pre * sig_p).astype(BF16)
     resid = nn(w_outT_ref[...], hidden) - (target - c_skip * x_full) / c_out
@@ -393,9 +418,164 @@
     pick = jnp.where(rows == 0, 1.0, jnp.where(rows == 1, c_noise, 0.0))
     small = nt(pick, dpre, precision=lax.Precision.HIGHEST)
     small = jnp.where(lax.broadcasted_iota(jnp.int32, (8, HID), 0) == 2, objective, small)
-    grad_ref[0:PDIM] = g_in
-    grad_ref[PDIM:2 * PDIM] = g_out
-    grad_ref[2 * PDIM:2 * PDIM + 8] = small
+
+    for h in range(2):
+        for k in range(3):
+            cols = slice(h * W + k * 128, h * W + k * 128 + 128)
+            grads[h, k * PDIM:(k + 1) * PDIM] = g_in[:, cols]
+            grads[h, (3 + k) * PDIM:(4 + k) * PDIM] = g_out[:, cols]
+            grads[h, 6 * PDIM + 8 * k:6 * PDIM + 8 * k + 8] = small[:, cols]
+        grads[h, 6 * PDIM + 24:] = jnp.zeros((PLANE * PIECE - 6 * PDIM - 24, 128), F32)
+
+    def piece(p):
+        return pl.ds(pl.multiple_of(p * PIECE, 8), PIECE)
+
+    def core_copy(p):
+        return rcopy(grads.at[1 - core, piece(p)], coreR.at[piece(p)], core_ss.at[p], core_rs.at[p], sib)
+
+    def plane_copy(k, p):
+        return pltpu.make_async_remote_copy(
+            src_ref=planeS.at[k], dst_ref=planeR.at[k], send_sem=plane_ss.at[k], recv_sem=plane_rs.at[k],
+            device_id=in_plane(p), device_id_type=MESH)
+
+    def start_core(k, _):
+        core_copy((me + k) % PLANE).start()
+        return 0
+
+    lax.fori_loop(1, PLANE + 1, start_core, 0)
+
+    def start_plane(k, _):
+        p = (me + k) % PLANE
+        core_copy(p).wait_recv()
+        planeS[k] = grads[core, piece(p)] + coreR[piece(p)]
+        plane_copy(k, p).start()
+        return 0
+
+    lax.fori_loop(1, PLANE, start_plane, 0)
+    core_copy(me).wait_recv()
+    planeR[0] = grads[core, piece(me)] + coreR[piece(me)]
+
+    def wait_plane(k, _):
+        plane_copy(k, (me + k) % PLANE).wait_recv()
+        planeR[0] += planeR[k]
+        return 0
+
+    lax.fori_loop(1, PLANE, wait_plane, 0)
+
+    def rows_of(o):
+        return pl.ds(pl.multiple_of(o * OWN, 8), OWN)
+
+    def z_copy(k, o):
+        return rcopy(planeR.at[0, rows_of(o)], zR.at[k], z_ss.at[k], z_rs.at[k], at(xl, o, core))
+
+    def back_copy(k, o):
+        view = whole.at[core, me, rows_of(o)]
+        return rcopy(view, view, back_ss.at[k], back_rs.at[o], at(xl, (z + k) % Z, core))
+
+    def start_z(k, _):
+        o = (z + k) % Z
+
+        @pl.when(o < OWNERS)
+        def _():
+            z_copy(k, o).start()
+
+        return 0
+
+    lax.fori_loop(1, Z, start_z, 0)
+
+    @pl.when(z < OWNERS)
+    def _():
+        zR[0] = planeR[0, rows_of(z)]
+
+        def wait_z(k, _):
+            z_copy(k, z).wait_recv()
+            zR[0] += zR[k]
+            return 0
+
+        lax.fori_loop(1, Z, wait_z, 0)
+        whole[core, me, rows_of(z)] = zR[0]
+
+        def start_back(k, _):
+            back_copy(k, z).start()
+            return 0
+
+        lax.fori_loop(1, Z, start_back, 0)
+
+    def wait_back(k, _):
+        o = (z + k) % Z
+
+        @pl.when(o < OWNERS)
+        def _():
+            back_copy(k, o).wait_recv()
+
+        return 0
+
+    lax.fori_loop(1, Z, wait_back, 0)
+
+    def share_copy(k, p, target):
+        return pltpu.make_async_remote_copy(
+            src_ref=whole.at[core, p], dst_ref=whole.at[core, p], send_sem=share_ss.at[k], recv_sem=share_rs.at[p],
+            device_id=in_plane(target), device_id_type=MESH)
+
+    def swap_whole(h, p):
+        return rcopy(whole.at[h, p], whole.at[h, p], swap2_ss.at[p], swap2_rs.at[p], sib)
+
+    def start_share(k, _):
+        share_copy(k, me, (me + k) % PLANE).start()
+        return 0
+
+    lax.fori_loop(1, PLANE, start_share, 0)
+    swap_whole(core, me).start()
+
+    def wait_share(k, _):
+        p = (me + PLANE - k) % PLANE
+        share_copy(k, p, (me + k) % PLANE).wait_recv()
+        swap_whole(core, p).start()
+        return 0
+
+    lax.fori_loop(1, PLANE, wait_share, 0)
+
+    def wait_swap(p, _):
+        swap_whole(1 - core, p).wait_recv()
+        return 0
+
+    lax.fori_loop(0, PLANE, wait_swap, 0)
+    for h in range(2):
+        flat = whole[h].reshape(PLANE * PIECE, 128)
+        for k in range(3):
+            cols = slice(h * W + k * 128, h * W + k * 128 + 128)
+            g_in_ref[:, cols] = flat[k * PDIM:(k + 1) * PDIM]
+            g_outT_ref[:, cols] = flat[(3 + k) * PDIM:(4 + k) * PDIM]
+            small_ref[:, cols] = flat[6 * PDIM + 8 * k:6 * PDIM + 8 * k + 8]
+
+    def grads_sent(k, _):
+        core_copy(k).wait_send()
+        swap_whole(core, k).wait_send()
+        return 0
+
+    lax.fori_loop(0, PLANE, grads_sent, 0)
+
+    def plane_sent(k, _):
+        plane_copy(k, (me + k) % PLANE).wait_send()
+        share_copy(k, me, (me + k) % PLANE).wait_send()
+        return 0
+
+    lax.fori_loop(1, PLANE, plane_sent, 0)
+
+    def z_sent(k, _):
+        o = (z + k) % Z
+
+        @pl.when(o < OWNERS)
+        def _():
+            z_copy(k, o).wait_send()
+
+        @pl.when(z < OWNERS)
+        def _():
+            back_copy(k, z).wait_send()
+
+        return 0
+
+    lax.fori_loop(1, Z, z_sent, 0)
 
     finish0()
     finish1()
@@ -426,17 +606,27 @@
             gbz(d, s, z).wait_send()
 
 
-def main_call(noise, refs, level, ids, w_in, bias, w_noise, w_outT):
+def main_call(noise, refs, level, ids, w_in, vec, w_outT):
     dma = pltpu.SemaphoreType.DMA
     vm = pltpu.VMEM
     any_spec = pl.BlockSpec(memory_space=pl.ANY)
     vmem_spec = pl.BlockSpec(memory_space=pltpu.VMEM)
     return pl.pallas_call(
         main_kernel,
-        out_shape=jax.ShapeDtypeStruct((2 * PDIM + 8, HID), F32),
-        in_specs=[any_spec] * 2 + [vmem_spec] * 6,
-        out_specs=vmem_spec,
+        out_shape=[
+            jax.ShapeDtypeStruct((PDIM, HID), F32),
+            jax.ShapeDtypeStruct((PDIM, HID), F32),
+            jax.ShapeDtypeStruct((8, HID), F32),
+        ],
+        in_specs=[any_spec] * 2 + [vmem_spec] * 5,
+        out_specs=[vmem_spec] * 3,
         scratch_shapes=[
+            vm((2, PLANE * PIECE, 128), F32),
+            vm((PLANE * PIECE, 128), F32),
+            vm((PLANE, PIECE, 128), F32),
+            vm((PLANE, PIECE, 128), F32),
+            vm((Z, OWN, 128), F32),
+            vm((2, PLANE, PIECE, 128), F32),
             vm((2 * Z, PAIR, W), BF16),
             vm((2 * Z, Q, W), F32),
             vm((Q, PAIR), BF16),
@@ -463,22 +653,20 @@
             dma((2, 2, 4)), dma((2, 2, 4)), dma((2,)), dma((2,)),
             dma((Z,)), dma((Z,)), dma((2, 4)), dma((2, 4)),
             dma((2, 4)), dma((2, 4)), dma((1,)), dma((1,)),
+            dma((PLANE,)), dma((PLANE,)), dma((PLANE,)), dma((PLANE,)), dma((Z,)), dma((Z,)),
+            dma((Z,)), dma((Z,)), dma((PLANE,)), dma((PLANE,)), dma((PLANE,)), dma((PLANE,)),
         ],
         compiler_params=pltpu.CompilerParams(
             collective_id=0, has_side_effects=True, vmem_limit_bytes=56 * 1024 * 1024),
         name="denoise_step",
-    )(noise, refs, level, ids, w_in, bias, w_noise, w_outT)
+    )(noise, refs, level, ids, w_in, vec, w_outT)
 
 
 def per_device(noise_field, ref_crops, level_index, query_ids, w_in, bias_hidden, w_noise, w_out):
-    grads = main_call(
+    g_in, g_outT, small = main_call(
         noise_field, ref_crops, level_index.reshape(1, Q), query_ids.reshape(1, Q), w_in,
-        bias_hidden.reshape(1, HID), w_noise.reshape(1, HID), w_out.T)
-    grads = lax.psum(grads, ("query", "ref"))
-    g_in = grads[0:PDIM]
-    g_out = grads[PDIM:2 * PDIM].T
-    small = grads[2 * PDIM:]
-    return (g_in, g_out, small[0], small[1], small[2, 0] / FEATS)
+        jnp.stack([bias_hidden, w_noise]), w_out.T)
+    return (g_in, g_outT.T, small[0], small[1], small[2, 0] / FEATS)
 
 
 def solution(mesh):

time: 399 us -> 166 us (0.42)
  waiting for transfers between devices: 258 us -> 0 us
  Pallas kernels: 116 us -> 155 us
  between operations: 15.8 us -> 2.43 us
    psum x1 -> x0, waiting for transfers between devices: 258 us -> none  [per_device(): grads = lax.psum(grads, ('query', 'ref'))]
    pallas_call x1, Pallas kernels: 116 us -> 155 us  [main_call(): pl.pallas_call(main_kernel, out_shape=[jax.ShapeDtypeStruct((PDIM, HID),...]
  transfers between devices with their start and end apart: 1 -> 0, of which waited for: 1 -> 0; matrix products, arithmetic and copies ran while one was open for 0% -> 0% of each run, Pallas kernels for 0% -> 0%
where the time goes in v2:
time: 166 us
  Pallas kernels  155 us (93%)
  local copies, waits for them, and re-layouts  7.83 us (5%)
  between operations  2.43 us (1%)
    pallas_call x1, Pallas kernels, main_call(): pl.pallas_call(main_kernel, out_shape=[jax.ShapeDtypeStruct((PDIM, HID),...  155 us
    unnamed x2, local copies, waits for them, and re-layouts  3.83 us

profile of v2, /device:TPU:1, one launch (start us, length us, event | category | flops | bytes accessed | tf_op | source)
XLA Modules:
  0.0 165.9 jit_solution(12611617387919196379)
XLA Ops:
  0.6 0.7 stack.10
  1.3 0.7 stack.9
  2.0 0.6 pad_maximum_fusion.vec_ref
  2.6 155.0 %denoise_step.1 = (f32[192,768]{1,0:T(8,128)}, f32[192,768]{1,0:T(8,128)}, f32[8,768]{1,0:T(8,128)}) custom-call(bf16[256,12288]{1,0:T(8,128)(2,1)} %noise_hbm.1, bf16[288,12288]{1,0:T(8,128)(2,1)} %refs_hbm.1, s32[1,256]{1,0:T(1,128)} %bitcast.7, s32[1,256]{1,0:T(1,128)} %bitcast.8, bf16[192,768]{1,0:T(8,128)(2,1)} %w_in_ref.1, ...), custom_call_target="tpu_custom_call" | custom-call | tf_op jit(solution)/shard_map/denoise_step/pallas_call | solution.py:614
  157.6 1.4 slice_reduce_fusion
  159.1 1.2 slice.11
  160.9 1.9 %copy.15 = f32[192,768]{1,0:T(8,128)} copy(f32[192,768]{1,0:T(8,128)} %get-tuple-element.18) | data formatting | bytes 1179648
  162.8 1.9 %copy.16 = f32[768,192]{0,1:T(8,128)} copy(f32[768,192]{0,1:T(8,128)} %bitcast.5) | data formatting | bytes 1179648

commit v3 on v2

--- a/solution.py
+++ b/solution.py
@@ -58,12 +58,15 @@
 
 
 def main_kernel(
-    noise_hbm, refs_hbm, level_ref, ids_ref, w_in_ref, vec_ref, w_outT_ref,
+    noise_hbm, refs_hbm, level_ref, ids_ref, w_in_hbm, bias_ref, w_noise_ref, w_outT_hbm,
     g_in_ref, g_outT_ref, small_ref,
     grads, coreR, planeS, planeR, zR, whole,
+    w_in_ref, w_outT_ref, scaled_ref, slope_ref, hidden_ref, fit_ref,
     refs, prod, match, noisy, noise, dots, halfS, halfR, statS, statR, sqacc,
+    xS, xR, zS, zR2, idsR, match2,
     axS, axR, azS, azR, bzS, bzR, bxS, bxR, shareS,
     local_sem, swap_ss, swap_rs, half_sem, stat_ss, stat_rs,
+    x_ss, x_rs, zz_ss, zz_rs, ids_sem,
     ax_ss, ax_rs, az_ss, az_rs, bz_ss, bz_rs, bx_ss, bx_rs,
     gax_ss, gax_rs, gaz_ss, gaz_rs, gbz_ss, gbz_rs, gbx_ss, gbx_rs,
     core_ss, core_rs, plane_ss, plane_rs, z_ss, z_rs, back_ss, back_rs, share_ss, share_rs, swap2_ss, swap2_rs,
@@ -128,6 +131,10 @@
     noise_copy = pltpu.make_async_copy(
         noise_hbm.at[:, pl.ds(noise_off, W)], noise, local_sem.at[2 * Z])
     noise_copy.start()
+    w_in_copy = pltpu.make_async_copy(w_in_hbm, w_in_ref, local_sem.at[2 * Z + 1])
+    w_out_copy = pltpu.make_async_copy(w_outT_hbm, w_outT_ref, local_sem.at[2 * Z + 2])
+    w_in_copy.start()
+    w_out_copy.start()
 
     barrier = pltpu.get_barrier_semaphore()
 
@@ -152,102 +159,186 @@
     lax.fori_loop(1, PLANE, greet_plane, 0)
     pl.semaphore_wait(barrier, CHIPS + PLANE - 2)
 
-    def start_swap(i, _):
+    sent = []
+
+    def start_swap(i):
         o = order(i)
         swap_copy(2 * o).start()
         swap_copy(2 * o + 1).start()
-        return 0
-
-    lax.fori_loop(0, Z, start_swap, 0)
+
+    xo = at(other, z, core)
+    q_xo = (1 - x_hi) * 4 + y
+    ids_copy = pltpu.make_async_remote_copy(
+        src_ref=ids_ref, dst_ref=idsR, send_sem=ids_sem.at[0], recv_sem=ids_sem.at[1],
+        device_id=(q_xo, xo), device_id_type=MESH)
+    ids_copy.start()
+    sent.append(ids_copy.wait_send)
+    for i in range(3):
+        start_swap(i)
+
+    def swap_sent():
+        def one(b, _):
+            swap_copy(b).wait_send()
+            return 0
+
+        lax.fori_loop(0, 2 * Z, one, 0)
+
+    sent.append(swap_sent)
 
     sigma = noise_level(level_ref[...])
     sigma_col = column(sigma)
-    ids = column(ids_ref[...].astype(F32)) - (chip * PAIR).astype(F32)
     places = lax.broadcasted_iota(jnp.int32, (Q, PAIR), 1).astype(F32)
-    match[...] = (ids == places).astype(F32).astype(BF16)
-
-    def reduce_scatter(ph):
+
+    def one_hot(row):
+        ids = column(row.astype(F32)) - (chip * PAIR).astype(F32)
+        return (ids == places).astype(F32).astype(BF16)
+
+    match[...] = one_hot(ids_ref[...])
+    match2[0:HALF] = match[0:HALF]
+
+    def x_copy(side, o):
+        return pltpu.make_async_remote_copy(
+            src_ref=xS.at[side, o], dst_ref=xR.at[side, o], send_sem=x_ss.at[side, o], recv_sem=x_rs.at[side, o],
+            device_id=(q if side == 0 else q_xo, xn), device_id_type=MESH)
+
+    def z_step(d, t):
+        rows = pl.ds(HALF * d, HALF) if t == 0 else slice(None)
+        return rcopy(zS.at[d, t, rows], zR2.at[d, t, rows], zz_ss.at[d, t], zz_rs.at[d, t], to[d])
+
+    def first_multiply(i):
+        o = order(i)
+        if i + 3 < Z:
+            start_swap(i + 3)
+        for j in range(2):
+            local_copy(2 * o + j).wait()
+            swap_landed(2 * o + j).wait_recv()
+        part = nn(match2[...], refs[2 * o + other]).astype(BF16)
+        for side in range(2):
+            xS[side, o] = part[side * HALF:(side + 1) * HALF]
+            x_copy(side, o).start()
+        prod[2 * o + xl] = nn(match[...], refs[2 * o + xl])
+
+    def first_sum(o, side):
+        x_copy(side, o).wait_recv()
+        return prod[2 * o + xl, side * HALF:(side + 1) * HALF] + xR[side, o].astype(F32)
+
+    def toward(d, t):
+        return (z + Z + (2 * d - 1) * (4 - t)) % Z
+
+    def first_reduce(idle):
+        for i in range(3):
+            first_multiply(i)
+        for d in range(2):
+            zS[d, 0, d * HALF:(d + 1) * HALF] = first_sum(toward(d, 0), d).astype(BF16)
+            z_step(d, 0).start()
+        for t in range(1, 4):
+            for i in range(2 * t + 1, min(2 * t + 3, Z)):
+                first_multiply(i)
+            idle(t)
+            for d in range(2):
+                z_step(d, t - 1).wait_recv()
+                for side in range(2):
+                    rows = slice(side * HALF, (side + 1) * HALF)
+                    part = first_sum(toward(d, t), side)
+                    if t > 1 or side == d:
+                        part = part + zR2[d, t - 1, rows].astype(F32)
+                    zS[d, t, rows] = part.astype(BF16)
+                z_step(d, t).start()
+        idle(0)
+        parts = [first_sum(z, side) for side in range(2)]
+        for d in range(2):
+            z_step(d, 3).wait_recv()
+            for side in range(2):
+                parts[side] = parts[side] + zR2[d, 3, side * HALF:(side + 1) * HALF].astype(F32)
+
+        def finish():
+            for d in range(2):
+                for t in range(4):
+                    z_step(d, t).wait_send()
+
+            def one(o, _):
+                x_copy(0, o).wait_send()
+                x_copy(1, o).wait_send()
+                return 0
+
+            lax.fori_loop(0, Z, one, 0)
+
+        sent.append(finish)
+        return parts
+
+    def reduce_scatter(idle):
         def ax(o):
-            return rcopy(axS.at[ph, o], axR.at[ph, o], ax_ss.at[ph, o], ax_rs.at[ph, o], xn)
+            return rcopy(axS.at[o], axR.at[o], ax_ss.at[o], ax_rs.at[o], xn)
 
         def az(d, t):
-            if t == 0:
-                rows = pl.ds(64 * d, 64)
-                return rcopy(azS.at[ph, d, 0, rows], azR.at[ph, d, 0, rows],
-                             az_ss.at[ph, d, 0], az_rs.at[ph, d, 0], to[d])
-            return rcopy(azS.at[ph, d, t], azR.at[ph, d, t],
-                         az_ss.at[ph, d, t], az_rs.at[ph, d, t], to[d])
+            rows = pl.ds(64 * d, 64) if t == 0 else slice(None)
+            return rcopy(azS.at[d, t, rows], azR.at[d, t, rows], az_ss.at[d, t], az_rs.at[d, t], to[d])
 
         def bz(d, t):
             if t == 0:
-                return rcopy(bzS.at[ph, d, 0, d], bzR.at[ph, d, 0, d],
-                             bz_ss.at[ph, d, 0], bz_rs.at[ph, d, 0], to[d])
-            return rcopy(bzS.at[ph, d, t], bzR.at[ph, d, t],
-                         bz_ss.at[ph, d, t], bz_rs.at[ph, d, t], to[d])
+                return rcopy(bzS.at[d, 0, d], bzR.at[d, 0, d], bz_ss.at[d, 0], bz_rs.at[d, 0], to[d])
+            return rcopy(bzS.at[d, t], bzR.at[d, t], bz_ss.at[d, t], bz_rs.at[d, t], to[d])
 
         def bx():
-            return rcopy(bxS.at[ph], bxR.at[ph], bx_ss.at[ph], bx_rs.at[ph], xn)
-
-        def multiply(i, _):
+            return rcopy(bxS, bxR, bx_ss.at[0], bx_rs.at[0], xn)
+
+        def multiply(i):
             o = order(i)
             for j in range(2):
-                b = 2 * o + j
-                if ph == 0:
-                    local_copy(b).wait()
-                    swap_landed(b).wait_recv()
-                prod[b] = nn(match[...], refs[b])
-            axS[ph, o] = prod[2 * o + other, 0:HALF].astype(BF16)
+                prod[2 * o + j] = nn(match[...], refs[2 * o + j])
+            axS[o] = prod[2 * o + other, 0:HALF].astype(BF16)
             ax(o).start()
-            return 0
-
-        multiply(0, 0)
-        o = order(0)
+
+        multiply(0)
         for d in range(2):
-            bzS[ph, d, 0, d] = prod[2 * o + d, HALF:Q].astype(BF16)
+            bzS[d, 0, d] = prod[2 * toward(d, 0) + d, HALF:Q].astype(BF16)
             bz(d, 0).start()
-        lax.fori_loop(1, Z, multiply, 0)
-
+        multiply(1)
+        multiply(2)
+        idle(0)
+        o = toward(0, 0)
         ax(o).wait_recv()
         for d in range(2):
             rows = slice(64 * d, 64 * d + 64)
-            azS[ph, d, 0, rows] = (prod[2 * o + xl, rows] + axR[ph, o, rows].astype(F32)).astype(BF16)
+            azS[d, 0, rows] = (prod[2 * o + xl, rows] + axR[o, rows].astype(F32)).astype(BF16)
             az(d, 0).start()
         for t in range(1, 4):
             for d in range(2):
-                o = (z + Z + (2 * d - 1) * (4 - t)) % Z
+                o = toward(d, t)
                 bz(d, t - 1).wait_recv()
                 for j in range(2):
                     s = prod[2 * o + j, HALF:Q]
                     if t > 1 or j == d:
-                        s = s + bzR[ph, d, t - 1, j].astype(F32)
-                    bzS[ph, d, t, j] = s.astype(BF16)
+                        s = s + bzR[d, t - 1, j].astype(F32)
+                    bzS[d, t, j] = s.astype(BF16)
                 bz(d, t).start()
+            for i in range(2 * t + 1, min(2 * t + 3, Z)):
+                multiply(i)
             for d in range(2):
-                o = (z + Z + (2 * d - 1) * (4 - t)) % Z
+                o = toward(d, t)
                 ax(o).wait_recv()
                 az(d, t - 1).wait_recv()
-                s = prod[2 * o + xl, 0:HALF] + axR[ph, o].astype(F32)
+                s = prod[2 * o + xl, 0:HALF] + axR[o].astype(F32)
                 if t > 1:
-                    azS[ph, d, t] = (s + azR[ph, d, t - 1].astype(F32)).astype(BF16)
+                    azS[d, t] = (s + azR[d, t - 1].astype(F32)).astype(BF16)
                 else:
-                    azS[ph, d, t] = s.astype(BF16)
+                    azS[d, t] = s.astype(BF16)
                     rows = slice(64 * d, 64 * d + 64)
-                    azS[ph, d, t, rows] = (s[rows] + azR[ph, d, 0, rows].astype(F32)).astype(BF16)
+                    azS[d, t, rows] = (s[rows] + azR[d, 0, rows].astype(F32)).astype(BF16)
                 az(d, t).start()
+            idle(t)
         for d in range(2):
             bz(d, 3).wait_recv()
-        bxS[ph] = (prod[2 * z + other, HALF:Q] + bzR[ph, 0, 3, other].astype(F32)
-                   + bzR[ph, 1, 3, other].astype(F32)).astype(BF16)
+        bxS[...] = (prod[2 * z + other, HALF:Q] + bzR[0, 3, other].astype(F32)
+                    + bzR[1, 3, other].astype(F32)).astype(BF16)
         bx().start()
         ax(z).wait_recv()
         for d in range(2):
             az(d, 3).wait_recv()
-        top = (prod[own, 0:HALF] + axR[ph, z].astype(F32)
-               + azR[ph, 0, 3].astype(F32) + azR[ph, 1, 3].astype(F32))
-        bottom = (prod[own, HALF:Q] + bzR[ph, 0, 3, xl].astype(F32)
-                  + bzR[ph, 1, 3, xl].astype(F32))
+        top = (prod[own, 0:HALF] + axR[z].astype(F32) + azR[0, 3].astype(F32) + azR[1, 3].astype(F32))
+        bottom = prod[own, HALF:Q] + bzR[0, 3, xl].astype(F32) + bzR[1, 3, xl].astype(F32)
         bx().wait_recv()
-        bottom = bottom + bxR[ph].astype(F32)
+        bottom = bottom + bxR[...].astype(F32)
 
         def finish():
             for d in range(2):
@@ -262,9 +353,24 @@
 
             lax.fori_loop(0, Z, one, 0)
 
-        return top, bottom, finish
-
-    top, bottom, finish0 = reduce_scatter(0)
+        sent.append(finish)
+        return top, bottom
+
+    sqacc[...] = jnp.zeros_like(sqacc)
+
+    def squares(t):
+        def one(b, _):
+            v = refs[b].astype(F32)
+            v = v * v
+            sqacc[...] += v[:, 0:128] + v[:, 128:256] + v[:, 256:384]
+            return 0
+
+        if t == 0:
+            lax.fori_loop(0, 2 * Z, one, 0)
+
+    ids_copy.wait_recv()
+    match2[HALF:Q] = one_hot(idsR[...])[HALF:Q]
+    top, bottom = first_reduce(squares)
     noise_copy.wait()
     noisy[own, 0:HALF] = (top + sigma_col[0:HALF] * noise[0:HALF].astype(F32)).astype(BF16)
     noisy[own, HALF:Q] = (bottom + sigma_col[HALF:Q] * noise[HALF:Q].astype(F32)).astype(BF16)
@@ -306,16 +412,6 @@
     gbx(other).wait_recv()
     for d in range(2):
         gbz(d, 1, z).start()
-
-    sqacc[...] = jnp.zeros_like(sqacc)
-
-    def squares(b, _):
-        v = refs[b].astype(F32)
-        v = v * v
-        sqacc[...] += v[:, 0:128] + v[:, 128:256] + v[:, 256:384]
-        return 0
-
-    lax.fori_loop(0, 2 * Z, squares, 0)
 
     for s in range(1, 4):
         for d in range(2):
@@ -335,6 +431,7 @@
                 o = came(d, s - 1)
                 gax(o, other).wait_recv()
                 score(o)
+    ref_sq = nt(jnp.ones((8, 128), F32), sqacc[...], precision=lax.Precision.HIGHEST)[0:1]
     o = came(0, 4)
     for d in range(2):
         gaz(d, 4, o).wait_recv()
@@ -347,10 +444,25 @@
     gax(o, other).wait_recv()
     score(o)
 
-    ref_sq = nt(jnp.ones((8, 128), F32), sqacc[...], precision=lax.Precision.HIGHEST)[0:1]
+    def gather_sent():
+        gbx(xl).wait_send()
+
+        def one(o, _):
+            gax(o, xl).wait_send()
+            return 0
+
+        lax.fori_loop(0, Z, one, 0)
+        for d in range(2):
+            for s in range(1, 5):
+                gaz(d, s, z).wait_send()
+                gbz(d, s, z).wait_send()
+
+    sent.append(gather_sent)
+
     halfS[...] = 2.0 * dots[...] - ref_sq
     half = rcopy(halfS, halfR, half_sem.at[0], half_sem.at[1], sib)
     half.start()
+    sent.append(half.wait_send)
     half.wait_recv()
     logits = (halfS[...] + halfR[...]) / (2.0 * sigma_col * sigma_col)
     dots[...] = logits
@@ -360,7 +472,7 @@
         return rcopy(statS.at[i], statR.at[i, k], stat_ss.at[i, k], stat_rs.at[i, k], peer)
 
     def tell(i, col):
-        statS[i] = row_of(col)
+        statS[i] = row_of(col)[0:1]
         statR[i, 0] = statS[i]
 
         def one(k, _):
@@ -368,6 +480,15 @@
             return 0
 
         lax.fori_loop(1, CHIPS, one, 0)
+
+        def told():
+            def one(k, _):
+                stat(i, k).wait_send()
+                return 0
+
+            lax.fori_loop(1, CHIPS, one, 0)
+
+        sent.append(told)
 
     def hear(i):
         def one(k, _):
@@ -376,18 +497,12 @@
 
         lax.fori_loop(1, CHIPS, one, 0)
 
-    tell(0, jnp.max(logits, axis=1, keepdims=True))
+    mine = jnp.max(logits, axis=1, keepdims=True)
+    tell(0, mine)
+    dots[...] = jnp.exp(logits - mine)
     hear(0)
-    peak = column(jnp.max(statR[0], axis=0)[0:1])
-    weights = jnp.exp(dots[...] - peak).astype(BF16)
-    match[...] = weights
-    tell(1, jnp.sum(weights.astype(F32), axis=1, keepdims=True))
-
-    top, bottom, finish1 = reduce_scatter(1)
-    shareS[0:HALF] = top
-    shareS[HALF:Q] = bottom
-    hear(1)
-    total = jnp.sum(statR[1], axis=0)[0:1]
+    peak = column(jnp.max(statR[0], axis=0))
+    match[...] = (dots[...] * jnp.exp(mine - peak)).astype(BF16)
 
     def patches(t):
         return jnp.concatenate([t[0:PDIM], t[PDIM:W]], axis=1)
@@ -395,54 +510,77 @@
     def twice(t):
         return jnp.concatenate([t, t], axis=1)
 
-    target = patches(shareS[...].T / total)
-    x_full = patches(noisy[own].astype(F32).T)
     s = twice(sigma)
     var = s * s + SIGMA_DATA * SIGMA_DATA
     c_skip = SIGMA_DATA * SIGMA_DATA / var
     c_out = s * SIGMA_DATA / jnp.sqrt(var)
     c_in = 1.0 / jnp.sqrt(var)
     c_noise = jnp.log(s) / 4.0
-    scaled = (c_in * x_full).astype(BF16)
-    pre = tn(w_in_ref[...], scaled) + column(vec_ref[1:2]) * c_noise + column(vec_ref[0:1])
-    sig_p = jax.nn.sigmoid(pre)
-    hidden = (pre * sig_p).astype(BF16)
-    resid = nn(w_outT_ref[...], hidden) - (target - c_skip * x_full) / c_out
+
+    def forward(t):
+        if t == 0:
+            tell(1, jnp.sum(match[...].astype(F32), axis=1, keepdims=True))
+            w_in_copy.wait()
+            w_out_copy.wait()
+        elif t == 1:
+            x_full = patches(noisy[own].astype(F32).T)
+            scaled = (c_in * x_full).astype(BF16)
+            scaled_ref[...] = scaled
+            fit_ref[...] = c_skip * x_full / c_out
+            slope_ref[...] = (tn(w_in_ref[...], scaled) + column(w_noise_ref[...].reshape(1, HID)) * c_noise
+                              + column(bias_ref[...].reshape(1, HID)))
+        elif t == 2:
+            pre = slope_ref[...]
+            sig_p = jax.nn.sigmoid(pre)
+            hidden_ref[...] = (pre * sig_p).astype(BF16)
+            slope_ref[...] = sig_p * (1.0 + pre * (1.0 - sig_p))
+        else:
+            fit_ref[...] += nn(w_outT_ref[...], hidden_ref[...])
+
+    top, bottom = reduce_scatter(forward)
+    shareS[0:HALF] = top
+    shareS[HALF:Q] = bottom
+    hear(1)
+    total = jnp.sum(statR[1], axis=0)
+
+    resid = fit_ref[...] - patches(shareS[...].T / total) / c_out
+    g_b = (2.0 / NQ * resid).astype(BF16)
+
+    def strips(at_row, value):
+        rows = value.shape[0]
+        for h in range(2):
+            for k in range(3):
+                cols = slice(h * W + k * 128, h * W + k * 128 + 128)
+                grads[h, at_row + k * rows:at_row + (k + 1) * rows] = value[:, cols]
+
+    def piece(p):
+        return pl.ds(pl.multiple_of(p * PIECE, 8), PIECE)
+
+    def core_copy(p):
+        return rcopy(grads.at[1 - core, piece(p)], coreR.at[piece(p)], core_ss.at[p], core_rs.at[p], sib)
+
+    def start_core(p, _):
+        core_copy(p).start()
+        return 0
+
+    early = 3 * PDIM // PIECE
+    strips(0, nt(g_b, hidden_ref[...]))
+    lax.fori_loop(0, early, start_core, 0)
+    dpre = tn(w_outT_ref[...], g_b) * slope_ref[...]
+    strips(3 * PDIM, nt(scaled_ref[...], dpre.astype(BF16)))
     objective = jnp.sum(resid * resid) / NQ
-    g_b = (2.0 / NQ * resid).astype(BF16)
-    g_out = nt(g_b, hidden)
-    back = tn(w_outT_ref[...], g_b)
-    dpre = back * sig_p * (1.0 + pre * (1.0 - sig_p))
-    g_in = nt(scaled, dpre.astype(BF16))
     rows = lax.broadcasted_iota(jnp.int32, (8, 2 * Q), 0)
     pick = jnp.where(rows == 0, 1.0, jnp.where(rows == 1, c_noise, 0.0))
     small = nt(pick, dpre, precision=lax.Precision.HIGHEST)
-    small = jnp.where(lax.broadcasted_iota(jnp.int32, (8, HID), 0) == 2, objective, small)
-
+    strips(6 * PDIM, jnp.where(lax.broadcasted_iota(jnp.int32, (8, HID), 0) == 2, objective, small))
     for h in range(2):
-        for k in range(3):
-            cols = slice(h * W + k * 128, h * W + k * 128 + 128)
-            grads[h, k * PDIM:(k + 1) * PDIM] = g_in[:, cols]
-            grads[h, (3 + k) * PDIM:(4 + k) * PDIM] = g_out[:, cols]
-            grads[h, 6 * PDIM + 8 * k:6 * PDIM + 8 * k + 8] = small[:, cols]
         grads[h, 6 * PDIM + 24:] = jnp.zeros((PLANE * PIECE - 6 * PDIM - 24, 128), F32)
-
-    def piece(p):
-        return pl.ds(pl.multiple_of(p * PIECE, 8), PIECE)
-
-    def core_copy(p):
-        return rcopy(grads.at[1 - core, piece(p)], coreR.at[piece(p)], core_ss.at[p], core_rs.at[p], sib)
+    lax.fori_loop(early, PLANE, start_core, 0)
 
     def plane_copy(k, p):
         return pltpu.make_async_remote_copy(
             src_ref=planeS.at[k], dst_ref=planeR.at[k], send_sem=plane_ss.at[k], recv_sem=plane_rs.at[k],
             device_id=in_plane(p), device_id_type=MESH)
-
-    def start_core(k, _):
-        core_copy((me + k) % PLANE).start()
-        return 0
-
-    lax.fori_loop(1, PLANE + 1, start_core, 0)
 
     def start_plane(k, _):
         p = (me + k) % PLANE
@@ -544,8 +682,8 @@
         flat = whole[h].reshape(PLANE * PIECE, 128)
         for k in range(3):
             cols = slice(h * W + k * 128, h * W + k * 128 + 128)
-            g_in_ref[:, cols] = flat[k * PDIM:(k + 1) * PDIM]
-            g_outT_ref[:, cols] = flat[(3 + k) * PDIM:(4 + k) * PDIM]
+            g_outT_ref[:, cols] = flat[k * PDIM:(k + 1) * PDIM]
+            g_in_ref[:, cols] = flat[(3 + k) * PDIM:(4 + k) * PDIM]
             small_ref[:, cols] = flat[6 * PDIM + 8 * k:6 * PDIM + 8 * k + 8]
 
     def grads_sent(k, _):
@@ -577,36 +715,11 @@
 
     lax.fori_loop(1, Z, z_sent, 0)
 
-    finish0()
-    finish1()
-
-    def swap_sent(b, _):
-        swap_copy(b).wait_send()
-        return 0
-
-    lax.fori_loop(0, 2 * Z, swap_sent, 0)
-    half.wait_send()
-
-    def stat_sent(k, _):
-        stat(0, k).wait_send()
-        stat(1, k).wait_send()
-        return 0
-
-    lax.fori_loop(1, CHIPS, stat_sent, 0)
-    gbx(xl).wait_send()
-
-    def gax_sent(o, _):
-        gax(o, xl).wait_send()
-        return 0
-
-    lax.fori_loop(0, Z, gax_sent, 0)
-    for d in range(2):
-        for s in range(1, 5):
-            gaz(d, s, z).wait_send()
-            gbz(d, s, z).wait_send()
-
-
-def main_call(noise, refs, level, ids, w_in, vec, w_outT):
+    for wait in sent:
+        wait()
+
+
+def main_call(noise, refs, level, ids, w_in, bias, w_noise, w_outT):
     dma = pltpu.SemaphoreType.DMA
     vm = pltpu.VMEM
     any_spec = pl.BlockSpec(memory_space=pl.ANY)
@@ -618,7 +731,7 @@
             jax.ShapeDtypeStruct((PDIM, HID), F32),
             jax.ShapeDtypeStruct((8, HID), F32),
         ],
-        in_specs=[any_spec] * 2 + [vmem_spec] * 5,
+        in_specs=[any_spec] * 2 + [vmem_spec] * 2 + [any_spec, vmem_spec, vmem_spec, any_spec],
         out_specs=[vmem_spec] * 3,
         scratch_shapes=[
             vm((2, PLANE * PIECE, 128), F32),
@@ -627,6 +740,12 @@
             vm((PLANE, PIECE, 128), F32),
             vm((Z, OWN, 128), F32),
             vm((2, PLANE, PIECE, 128), F32),
+            vm((PDIM, HID), BF16),
+            vm((PDIM, HID), BF16),
+            vm((PDIM, 2 * Q), BF16),
+            vm((HID, 2 * Q), F32),
+            vm((HID, 2 * Q), BF16),
+            vm((PDIM, 2 * Q), F32),
             vm((2 * Z, PAIR, W), BF16),
             vm((2 * Z, Q, W), F32),
             vm((Q, PAIR), BF16),
@@ -635,22 +754,29 @@
             vm((Q, PAIR), F32),
             vm((Q, PAIR), F32),
             vm((Q, PAIR), F32),
-            vm((2, 8, Q), F32),
-            vm((2, CHIPS, 8, Q), F32),
+            vm((2, 1, Q), F32),
+            vm((2, CHIPS, 1, Q), F32),
             vm((PAIR, 128), F32),
             vm((2, Z, HALF, W), BF16),
             vm((2, Z, HALF, W), BF16),
-            vm((2, 2, 4, HALF, W), BF16),
-            vm((2, 2, 4, HALF, W), BF16),
-            vm((2, 2, 4, 2, HALF, W), BF16),
-            vm((2, 2, 4, 2, HALF, W), BF16),
-            vm((2, HALF, W), BF16),
-            vm((2, HALF, W), BF16),
+            vm((2, 4, Q, W), BF16),
+            vm((2, 4, Q, W), BF16),
+            vm((1, Q), jnp.int32),
+            vm((Q, PAIR), BF16),
+            vm((Z, HALF, W), BF16),
+            vm((Z, HALF, W), BF16),
+            vm((2, 4, HALF, W), BF16),
+            vm((2, 4, HALF, W), BF16),
+            vm((2, 4, 2, HALF, W), BF16),
+            vm((2, 4, 2, HALF, W), BF16),
+            vm((HALF, W), BF16),
+            vm((HALF, W), BF16),
             vm((Q, W), F32),
-            dma((2 * Z + 1,)), dma((2 * Z,)), dma((2 * Z,)), dma((2,)),
+            dma((2 * Z + 3,)), dma((2 * Z,)), dma((2 * Z,)), dma((2,)),
             dma((2, CHIPS)), dma((2, CHIPS)),
-            dma((2, Z)), dma((2, Z)), dma((2, 2, 4)), dma((2, 2, 4)),
-            dma((2, 2, 4)), dma((2, 2, 4)), dma((2,)), dma((2,)),
+            dma((2, Z)), dma((2, Z)), dma((2, 4)), dma((2, 4)), dma((2,)),
+            dma((Z,)), dma((Z,)), dma((2, 4)), dma((2, 4)),
+            dma((2, 4)), dma((2, 4)), dma((1,)), dma((1,)),
             dma((Z,)), dma((Z,)), dma((2, 4)), dma((2, 4)),
             dma((2, 4)), dma((2, 4)), dma((1,)), dma((1,)),
             dma((PLANE,)), dma((PLANE,)), dma((PLANE,)), dma((PLANE,)), dma((Z,)), dma((Z,)),
@@ -659,14 +785,35 @@
         compiler_params=pltpu.CompilerParams(
             collective_id=0, has_side_effects=True, vmem_limit_bytes=56 * 1024 * 1024),
         name="denoise_step",
-    )(noise, refs, level, ids, w_in, vec, w_outT)
+    )(noise, refs, level, ids, w_in, bias, w_noise, w_outT)
+
+
+def write_kernel(g_in_ref, g_outT_ref, small_ref, g_in_out, g_outT_out, bias_out, noise_out, loss_out):
+    g_in_out[...] = g_in_ref[...]
+    g_outT_out[...] = g_outT_ref[...]
+    bias_out[...] = small_ref[0]
+    noise_out[...] = small_ref[1]
+    loss_out[...] = small_ref[2:3, 0:1] * (1.0 / FEATS)
+
+
+def write_call(g_in, g_outT, small):
+    vmem_spec = pl.BlockSpec(memory_space=pltpu.VMEM)
+    shape = jax.ShapeDtypeStruct
+    return pl.pallas_call(
+        write_kernel,
+        out_shape=[shape((PDIM, HID), F32)] * 2 + [shape((HID,), F32)] * 2 + [shape((1, 1), F32)],
+        in_specs=[vmem_spec] * 3,
+        out_specs=[vmem_spec] * 5,
+        name="write_results",
+    )(g_in, g_outT, small)
 
 
 def per_device(noise_field, ref_crops, level_index, query_ids, w_in, bias_hidden, w_noise, w_out):
     g_in, g_outT, small = main_call(
         noise_field, ref_crops, level_index.reshape(1, Q), query_ids.reshape(1, Q), w_in,
-        jnp.stack([bias_hidden, w_noise]), w_out.T)
-    return (g_in, g_outT.T, small[0], small[1], small[2, 0] / FEATS)
+        bias_hidden, w_noise, w_out.T)
+    g_in, g_outT, bias, w_noise, loss = write_call(g_in, g_outT, small)
+    return (g_in, g_outT.T, bias, w_noise, loss.reshape(()))
 
 
 def solution(mesh):

time: 166 us -> 154 us (0.928)
  local copies, waits for them, and re-layouts: 7.83 us -> 0 us
  Pallas kernels: 155 us -> 153 us
  between operations: 2.43 us -> 0.64 us
    pallas_call x1, Pallas kernels: 155 us -> 151 us  [main_call(): pl.pallas_call(main_kernel, out_shape=[jax.ShapeDtypeStruct((PDIM, HID),...]
    unnamed x2 -> x0, local copies, waits for them, and re-layouts: 3.83 us -> none
    slice x2 -> x0, local copies, waits for them, and re-layouts: 2.61 us -> none  [per_device(): return (g_in, g_outT.T, small[0], small[1], small[2, 0] / FEATS)]
    pallas_call x0 -> x1, Pallas kernels: none -> 2.3 us  [write_call(): pl.pallas_call(write_kernel, out_shape=[shape((PDIM, HID), F32)] * 2 + [s...]
where the time goes in v3:
time: 154 us
  Pallas kernels  153 us (99%)
    pallas_call x1, Pallas kernels, main_call(): pl.pallas_call(main_kernel, out_shape=[jax.ShapeDtypeStruct((PDIM, HID),...  151 us

profile of v3, /device:TPU:1, one launch (start us, length us, event | category | flops | bytes accessed | tf_op | source)
XLA Modules:
  0.0 153.6 jit_solution(13924937761780190894)
XLA Ops:
  0.6 150.6 %denoise_step.1 = (f32[192,768]{1,0:T(8,128)}, f32[192,768]{1,0:T(8,128)}, f32[8,768]{1,0:T(8,128)}) custom-call(bf16[256,12288]{1,0:T(8,128)(2,1)} %noise_hbm.1, bf16[288,12288]{1,0:T(8,128)(2,1)} %refs_hbm.1, s32[1,256]{1,0:T(1,128)} %bitcast.6, s32[1,256]{1,0:T(1,128)} %bitcast.7, bf16[192,768]{1,0:T(8,128)(2,1)} %w_in_hbm.1, f32[768]{0:T(1024)} %bias_ref.1, ...), custom_call_target="tpu_custom_call" | custom-call | tf_op jit(solution)/shard_map/denoise_step/pallas_call | solution.py:727
  151.3 2.3 %write_results.1 = (f32[192,768]{1,0:T(8,128)}, f32[192,768]{1,0:T(8,128)}, f32[768]{0:T(1024)}, f32[768]{0:T(1024)}, f32[1,1]{1,0:T(1,128)}) custom-call(f32[192,768]{1,0:T(8,128)} %get-tuple-element.13.g_in_ref, f32[192,768]{1,0:T(8,128)} %get-tuple-element.14.g_outT_ref, f32[8,768]{1,0:T(8,128)} %get-tuple-element.15.small_ref), custom_call_target="tpu_custom_call" | custom-call | tf_op jit(solution)/shard_map/write_results/pallas_call | solution.py:802

commit v4 on v3

--- a/solution.py
+++ b/solution.py
@@ -23,9 +23,10 @@
 NQ = 2048
 FEATS = 12288
 PLANE = 16
-PIECE = 80
-OWN = 16
-OWNERS = PIECE // OWN
+PP = 48
+RP = 64
+P_ROWS = PLANE * PP
+ROWS = P_ROWS + Z * RP
 
 
 def nt(a, b, **kw):
@@ -60,7 +61,7 @@
 def main_kernel(
     noise_hbm, refs_hbm, level_ref, ids_ref, w_in_hbm, bias_ref, w_noise_ref, w_outT_hbm,
     g_in_ref, g_outT_ref, small_ref,
-    grads, coreR, planeS, planeR, zR, whole,
+    grads, coreR, pS, pR, pzR, rS, rR, rxR, ryR, wholeP, wholeR,
     w_in_ref, w_outT_ref, scaled_ref, slope_ref, hidden_ref, fit_ref,
     refs, prod, match, noisy, noise, dots, halfS, halfR, statS, statR, sqacc,
     xS, xR, zS, zR2, idsR, match2,
@@ -69,7 +70,8 @@
     x_ss, x_rs, zz_ss, zz_rs, ids_sem,
     ax_ss, ax_rs, az_ss, az_rs, bz_ss, bz_rs, bx_ss, bx_rs,
     gax_ss, gax_rs, gaz_ss, gaz_rs, gbz_ss, gbz_rs, gbx_ss, gbx_rs,
-    core_ss, core_rs, plane_ss, plane_rs, z_ss, z_rs, back_ss, back_rs, share_ss, share_rs, swap2_ss, swap2_rs,
+    core_ss, core_rs, pp_ss, pp_rs, rz_ss, rz_rs, pz_ss, pz_rs, rx_ss, rx_rs, ry_ss, ry_rs,
+    pshare_ss, pshare_rs, rshare_ss, rshare_rs, trade_ss, trade_rs,
 ):
     q = lax.axis_index("query")
     r = lax.axis_index("ref")
@@ -553,168 +555,153 @@
                 cols = slice(h * W + k * 128, h * W + k * 128 + 128)
                 grads[h, at_row + k * rows:at_row + (k + 1) * rows] = value[:, cols]
 
-    def piece(p):
-        return pl.ds(pl.multiple_of(p * PIECE, 8), PIECE)
-
-    def core_copy(p):
-        return rcopy(grads.at[1 - core, piece(p)], coreR.at[piece(p)], core_ss.at[p], core_rs.at[p], sib)
-
-    def start_core(p, _):
-        core_copy(p).start()
-        return 0
-
-    early = 3 * PDIM // PIECE
+    def core_copy(i):
+        rows = (pl.ds(0, P_ROWS), pl.ds(P_ROWS, Z * RP))[i]
+        return rcopy(grads.at[1 - core, rows], coreR.at[rows], core_ss.at[i], core_rs.at[i], sib)
+
+    def loop(first, last, body):
+        def one(k, _):
+            body(k)
+            return 0
+
+        lax.fori_loop(first, last, one, 0)
+
+    def plane_copy(src, dst, ssem, rsem, p):
+        return pltpu.make_async_remote_copy(
+            src_ref=src, dst_ref=dst, send_sem=ssem, recv_sem=rsem, device_id=in_plane(p), device_id_type=MESH)
+
+    def z_copy(src, dst, ssem, rsem, o):
+        return rcopy(src, dst, ssem, rsem, at(xl, o, core))
+
+    x = me // 4
+
+    def pp(k):
+        p = (me + k) % PLANE
+        return plane_copy(pS.at[p], pR.at[k], pp_ss.at[k], pp_rs.at[k], p)
+
+    def rz(k):
+        o = (z + k) % Z
+        return z_copy(rS.at[o], rR.at[k], rz_ss.at[k], rz_rs.at[k], o)
+
+    def pz(k, origin):
+        view = pzR.at[origin]
+        return z_copy(view, view, pz_ss.at[k], pz_rs.at[origin], (z + k) % Z)
+
+    def rx(k, origin):
+        view = rxR.at[origin]
+        return plane_copy(view, view, rx_ss.at[k], rx_rs.at[origin], ((x + k) % 4) * 4 + y)
+
+    def ry(k, origin):
+        view = ryR.at[origin]
+        return plane_copy(view, view, ry_ss.at[k], ry_rs.at[origin], x * 4 + (y + k) % 4)
+
+    def pshare(k, p):
+        view = wholeP.at[core, p]
+        return plane_copy(view, view, pshare_ss.at[k], pshare_rs.at[p], (me + k) % PLANE)
+
+    def rshare(k, o):
+        view = wholeR.at[core, o]
+        return z_copy(view, view, rshare_ss.at[k], rshare_rs.at[o], (z + k) % Z)
+
+    def ptrade(h, p):
+        return rcopy(wholeP.at[h, p], wholeP.at[h, p], trade_ss.at[p], trade_rs.at[p], sib)
+
+    def rtrade(h, o):
+        return rcopy(wholeR.at[h, o], wholeR.at[h, o], trade_ss.at[PLANE + o], trade_rs.at[PLANE + o], sib)
+
     strips(0, nt(g_b, hidden_ref[...]))
-    lax.fori_loop(0, early, start_core, 0)
     dpre = tn(w_outT_ref[...], g_b) * slope_ref[...]
     strips(3 * PDIM, nt(scaled_ref[...], dpre.astype(BF16)))
+    core_copy(0).start()
     objective = jnp.sum(resid * resid) / NQ
     rows = lax.broadcasted_iota(jnp.int32, (8, 2 * Q), 0)
     pick = jnp.where(rows == 0, 1.0, jnp.where(rows == 1, c_noise, 0.0))
     small = nt(pick, dpre, precision=lax.Precision.HIGHEST)
     strips(6 * PDIM, jnp.where(lax.broadcasted_iota(jnp.int32, (8, HID), 0) == 2, objective, small))
     for h in range(2):
-        grads[h, 6 * PDIM + 24:] = jnp.zeros((PLANE * PIECE - 6 * PDIM - 24, 128), F32)
-    lax.fori_loop(early, PLANE, start_core, 0)
-
-    def plane_copy(k, p):
-        return pltpu.make_async_remote_copy(
-            src_ref=planeS.at[k], dst_ref=planeR.at[k], send_sem=plane_ss.at[k], recv_sem=plane_rs.at[k],
-            device_id=in_plane(p), device_id_type=MESH)
-
-    def start_plane(k, _):
-        p = (me + k) % PLANE
-        core_copy(p).wait_recv()
-        planeS[k] = grads[core, piece(p)] + coreR[piece(p)]
-        plane_copy(k, p).start()
-        return 0
-
-    lax.fori_loop(1, PLANE, start_plane, 0)
-    core_copy(me).wait_recv()
-    planeR[0] = grads[core, piece(me)] + coreR[piece(me)]
-
-    def wait_plane(k, _):
-        plane_copy(k, (me + k) % PLANE).wait_recv()
-        planeR[0] += planeR[k]
-        return 0
-
-    lax.fori_loop(1, PLANE, wait_plane, 0)
-
-    def rows_of(o):
-        return pl.ds(pl.multiple_of(o * OWN, 8), OWN)
-
-    def z_copy(k, o):
-        return rcopy(planeR.at[0, rows_of(o)], zR.at[k], z_ss.at[k], z_rs.at[k], at(xl, o, core))
-
-    def back_copy(k, o):
-        view = whole.at[core, me, rows_of(o)]
-        return rcopy(view, view, back_ss.at[k], back_rs.at[o], at(xl, (z + k) % Z, core))
-
-    def start_z(k, _):
-        o = (z + k) % Z
-
-        @pl.when(o < OWNERS)
-        def _():
-            z_copy(k, o).start()
-
-        return 0
-
-    lax.fori_loop(1, Z, start_z, 0)
-
-    @pl.when(z < OWNERS)
-    def _():
-        zR[0] = planeR[0, rows_of(z)]
-
-        def wait_z(k, _):
-            z_copy(k, z).wait_recv()
-            zR[0] += zR[k]
-            return 0
-
-        lax.fori_loop(1, Z, wait_z, 0)
-        whole[core, me, rows_of(z)] = zR[0]
-
-        def start_back(k, _):
-            back_copy(k, z).start()
-            return 0
-
-        lax.fori_loop(1, Z, start_back, 0)
-
-    def wait_back(k, _):
-        o = (z + k) % Z
-
-        @pl.when(o < OWNERS)
-        def _():
-            back_copy(k, o).wait_recv()
-
-        return 0
-
-    lax.fori_loop(1, Z, wait_back, 0)
-
-    def share_copy(k, p, target):
-        return pltpu.make_async_remote_copy(
-            src_ref=whole.at[core, p], dst_ref=whole.at[core, p], send_sem=share_ss.at[k], recv_sem=share_rs.at[p],
-            device_id=in_plane(target), device_id_type=MESH)
-
-    def swap_whole(h, p):
-        return rcopy(whole.at[h, p], whole.at[h, p], swap2_ss.at[p], swap2_rs.at[p], sib)
-
-    def start_share(k, _):
-        share_copy(k, me, (me + k) % PLANE).start()
-        return 0
-
-    lax.fori_loop(1, PLANE, start_share, 0)
-    swap_whole(core, me).start()
-
-    def wait_share(k, _):
+        grads[h, 6 * PDIM + 24:] = jnp.zeros((ROWS - 6 * PDIM - 24, 128), F32)
+    core_copy(1).start()
+    core_copy(0).wait_recv()
+    pS[...] = (grads[core, 0:P_ROWS] + coreR[0:P_ROWS]).reshape(PLANE, PP, 128)
+    loop(1, PLANE, lambda k: pp(k).start())
+    core_copy(1).wait_recv()
+    rS[...] = (grads[core, P_ROWS:] + coreR[P_ROWS:]).reshape(Z, RP, 128)
+    loop(1, Z, lambda k: rz(k).start())
+
+    pR[0] = pS[me]
+
+    def add_pp(k):
+        pp(k).wait_recv()
+        pR[0] += pR[k]
+
+    loop(1, PLANE, add_pp)
+    pzR[z] = pR[0]
+    loop(1, Z, lambda k: pz(k, z).start())
+    rR[0] = rS[z]
+
+    def add_rz(k):
+        rz(k).wait_recv()
+        rR[0] += rR[k]
+
+    loop(1, Z, add_rz)
+    rxR[x] = rR[0]
+    loop(1, 4, lambda k: rx(k, x).start())
+    loop(1, 4, lambda k: rx(k, (x + k) % 4).wait_recv())
+    ryR[y] = jnp.sum(rxR[...], axis=0)
+    loop(1, 4, lambda k: ry(k, y).start())
+    loop(1, Z, lambda k: pz(k, (z + k) % Z).wait_recv())
+    wholeP[core, me] = jnp.sum(pzR[...], axis=0)
+    loop(1, PLANE, lambda k: pshare(k, me).start())
+    loop(1, 4, lambda k: ry(k, (y + k) % 4).wait_recv())
+    wholeR[core, z] = jnp.sum(ryR[...], axis=0)
+    loop(1, Z, lambda k: rshare(k, z).start())
+    ptrade(core, me).start()
+    rtrade(core, z).start()
+
+    def pass_r(k):
+        o = (z + Z - k) % Z
+        rshare(k, o).wait_recv()
+        rtrade(core, o).start()
+
+    def pass_p(k):
         p = (me + PLANE - k) % PLANE
-        share_copy(k, p, (me + k) % PLANE).wait_recv()
-        swap_whole(core, p).start()
-        return 0
-
-    lax.fori_loop(1, PLANE, wait_share, 0)
-
-    def wait_swap(p, _):
-        swap_whole(1 - core, p).wait_recv()
-        return 0
-
-    lax.fori_loop(0, PLANE, wait_swap, 0)
+        pshare(k, p).wait_recv()
+        ptrade(core, p).start()
+
+    loop(1, Z, pass_r)
+    loop(1, PLANE, pass_p)
+    loop(0, Z, lambda o: rtrade(1 - core, o).wait_recv())
+    loop(0, PLANE, lambda p: ptrade(1 - core, p).wait_recv())
     for h in range(2):
-        flat = whole[h].reshape(PLANE * PIECE, 128)
+        first = wholeP[h].reshape(P_ROWS, 128)
+        second = wholeR[h].reshape(Z * RP, 128)
         for k in range(3):
             cols = slice(h * W + k * 128, h * W + k * 128 + 128)
-            g_outT_ref[:, cols] = flat[k * PDIM:(k + 1) * PDIM]
-            g_in_ref[:, cols] = flat[(3 + k) * PDIM:(4 + k) * PDIM]
-            small_ref[:, cols] = flat[6 * PDIM + 8 * k:6 * PDIM + 8 * k + 8]
-
-    def grads_sent(k, _):
-        core_copy(k).wait_send()
-        swap_whole(core, k).wait_send()
-        return 0
-
-    lax.fori_loop(0, PLANE, grads_sent, 0)
-
-    def plane_sent(k, _):
-        plane_copy(k, (me + k) % PLANE).wait_send()
-        share_copy(k, me, (me + k) % PLANE).wait_send()
-        return 0
-
-    lax.fori_loop(1, PLANE, plane_sent, 0)
-
-    def z_sent(k, _):
-        o = (z + k) % Z
-
-        @pl.when(o < OWNERS)
-        def _():
-            z_copy(k, o).wait_send()
-
-        @pl.when(z < OWNERS)
-        def _():
-            back_copy(k, z).wait_send()
-
-        return 0
-
-    lax.fori_loop(1, Z, z_sent, 0)
-
+            g_outT_ref[:, cols] = first[k * PDIM:(k + 1) * PDIM]
+            g_in_ref[:, cols] = first[3 * PDIM:] if k == 0 else second[(k - 1) * PDIM:k * PDIM]
+            small_ref[:, cols] = second[2 * PDIM + 8 * k:2 * PDIM + 8 * k + 8]
+
+    for i in range(2):
+        core_copy(i).wait_send()
+    loop(0, PLANE, lambda p: ptrade(core, p).wait_send())
+    loop(0, Z, lambda o: rtrade(core, o).wait_send())
+
+    def plane_sent(k):
+        pp(k).wait_send()
+        pshare(k, me).wait_send()
+
+    def z_sent(k):
+        rz(k).wait_send()
+        pz(k, z).wait_send()
+        rshare(k, z).wait_send()
+
+    def side_sent(k):
+        rx(k, x).wait_send()
+        ry(k, y).wait_send()
+
+    loop(1, PLANE, plane_sent)
+    loop(1, Z, z_sent)
+    loop(1, 4, side_sent)
     for wait in sent:
         wait()
 
@@ -734,12 +721,17 @@
         in_specs=[any_spec] * 2 + [vmem_spec] * 2 + [any_spec, vmem_spec, vmem_spec, any_spec],
         out_specs=[vmem_spec] * 3,
         scratch_shapes=[
-            vm((2, PLANE * PIECE, 128), F32),
-            vm((PLANE * PIECE, 128), F32),
-            vm((PLANE, PIECE, 128), F32),
-            vm((PLANE, PIECE, 128), F32),
-            vm((Z, OWN, 128), F32),
-            vm((2, PLANE, PIECE, 128), F32),
+            vm((2, ROWS, 128), F32),
+            vm((ROWS, 128), F32),
+            vm((PLANE, PP, 128), F32),
+            vm((PLANE, PP, 128), F32),
+            vm((Z, PP, 128), F32),
+            vm((Z, RP, 128), F32),
+            vm((Z, RP, 128), F32),
+            vm((4, RP, 128), F32),
+            vm((4, RP, 128), F32),
+            vm((2, PLANE, PP, 128), F32),
+            vm((2, Z, RP, 128), F32),
             vm((PDIM, HID), BF16),
             vm((PDIM, HID), BF16),
             vm((PDIM, 2 * Q), BF16),
@@ -779,8 +771,9 @@
             dma((2, 4)), dma((2, 4)), dma((1,)), dma((1,)),
             dma((Z,)), dma((Z,)), dma((2, 4)), dma((2, 4)),
             dma((2, 4)), dma((2, 4)), dma((1,)), dma((1,)),
-            dma((PLANE,)), dma((PLANE,)), dma((PLANE,)), dma((PLANE,)), dma((Z,)), dma((Z,)),
-            dma((Z,)), dma((Z,)), dma((PLANE,)), dma((PLANE,)), dma((PLANE,)), dma((PLANE,)),
+            dma((2,)), dma((2,)), dma((PLANE,)), dma((PLANE,)), dma((Z,)), dma((Z,)),
+            dma((Z,)), dma((Z,)), dma((4,)), dma((4,)), dma((4,)), dma((4,)),
+            dma((PLANE,)), dma((PLANE,)), dma((Z,)), dma((Z,)), dma((PLANE + Z,)), dma((PLANE + Z,)),
         ],
         compiler_params=pltpu.CompilerParams(
             collective_id=0, has_side_effects=True, vmem_limit_bytes=56 * 1024 * 1024),

time: 154 us -> 150 us (0.974)
  Pallas kernels: 153 us -> 149 us
    pallas_call x1, Pallas kernels: 151 us -> 147 us  [main_call(): pl.pallas_call(main_kernel, out_shape=[jax.ShapeDtypeStruct((PDIM, HID),...]
where the time goes in v4:
time: 150 us
  Pallas kernels  149 us (99%)
    pallas_call x1, Pallas kernels, main_call(): pl.pallas_call(main_kernel, out_shape=[jax.ShapeDtypeStruct((PDIM, HID),...  147 us

profile of v4, /device:TPU:1, one launch (start us, length us, event | category | flops | bytes accessed | tf_op | source)
XLA Modules:
  0.0 149.8 jit_solution(3098638452093832005)
XLA Ops:
  0.6 146.8 %denoise_step.1 = (f32[192,768]{1,0:T(8,128)}, f32[192,768]{1,0:T(8,128)}, f32[8,768]{1,0:T(8,128)}) custom-call(bf16[256,12288]{1,0:T(8,128)(2,1)} %noise_hbm.1, bf16[288,12288]{1,0:T(8,128)(2,1)} %refs_hbm.1, s32[1,256]{1,0:T(1,128)} %bitcast.6, s32[1,256]{1,0:T(1,128)} %bitcast.7, bf16[192,768]{1,0:T(8,128)(2,1)} %w_in_hbm.1, f32[768]{0:T(1024)} %bias_ref.1, ...), custom_call_target="tpu_custom_call" | custom-call | tf_op jit(solution)/shard_map/denoise_step/pallas_call | solution.py:714
  147.5 2.3 %write_results.1 = (f32[192,768]{1,0:T(8,128)}, f32[192,768]{1,0:T(8,128)}, f32[768]{0:T(1024)}, f32[768]{0:T(1024)}, f32[1,1]{1,0:T(1,128)}) custom-call(f32[192,768]{1,0:T(8,128)} %get-tuple-element.13.g_in_ref, f32[192,768]{1,0:T(8,128)} %get-tuple-element.14.g_outT_ref, f32[8,768]{1,0:T(8,128)} %get-tuple-element.15.small_ref), custom_call_target="tpu_custom_call" | custom-call | tf_op jit(solution)/shard_map/write_results/pallas_call | solution.py:795

commit v5 on v4

--- a/solution.py
+++ b/solution.py
@@ -15,6 +15,9 @@
 CHIPS = 2 * Z
 Q = 256
 HALF = 128
+NA = 160
+NB = Q - NA
+NA0 = 80
 REF = 288
 PAIR = 2 * REF
 W = 384
@@ -203,9 +206,9 @@
             src_ref=xS.at[side, o], dst_ref=xR.at[side, o], send_sem=x_ss.at[side, o], recv_sem=x_rs.at[side, o],
             device_id=(q if side == 0 else q_xo, xn), device_id_type=MESH)
 
-    def z_step(d, t):
-        rows = pl.ds(HALF * d, HALF) if t == 0 else slice(None)
-        return rcopy(zS.at[d, t, rows], zR2.at[d, t, rows], zz_ss.at[d, t], zz_rs.at[d, t], to[d])
+    def z_step(d, t, side):
+        rows = pl.ds(HALF * side, HALF)
+        return rcopy(zS.at[d, t, rows], zR2.at[d, t, rows], zz_ss.at[d, t, side], zz_rs.at[d, t, side], to[d])
 
     def first_multiply(i):
         o = order(i)
@@ -227,36 +230,41 @@
     def toward(d, t):
         return (z + Z + (2 * d - 1) * (4 - t)) % Z
 
+    def opposite(d):
+        return pl.ds(NA0 * d, (NA0, NA - NA0)[d])
+
     def first_reduce(idle):
         for i in range(3):
             first_multiply(i)
         for d in range(2):
             zS[d, 0, d * HALF:(d + 1) * HALF] = first_sum(toward(d, 0), d).astype(BF16)
-            z_step(d, 0).start()
+            z_step(d, 0, d).start()
         for t in range(1, 4):
             for i in range(2 * t + 1, min(2 * t + 3, Z)):
                 first_multiply(i)
             idle(t)
-            for d in range(2):
-                z_step(d, t - 1).wait_recv()
-                for side in range(2):
-                    rows = slice(side * HALF, (side + 1) * HALF)
+            for side in range(2):
+                rows = slice(side * HALF, (side + 1) * HALF)
+                for d in range(2):
                     part = first_sum(toward(d, t), side)
                     if t > 1 or side == d:
+                        z_step(d, t - 1, side).wait_recv()
                         part = part + zR2[d, t - 1, rows].astype(F32)
                     zS[d, t, rows] = part.astype(BF16)
-                z_step(d, t).start()
+                    z_step(d, t, side).start()
         idle(0)
         parts = [first_sum(z, side) for side in range(2)]
-        for d in range(2):
-            z_step(d, 3).wait_recv()
-            for side in range(2):
+        for side in range(2):
+            for d in range(2):
+                z_step(d, 3, side).wait_recv()
                 parts[side] = parts[side] + zR2[d, 3, side * HALF:(side + 1) * HALF].astype(F32)
 
         def finish():
             for d in range(2):
-                for t in range(4):
-                    z_step(d, t).wait_send()
+                z_step(d, 0, d).wait_send()
+                for t in range(1, 4):
+                    for side in range(2):
+                        z_step(d, t, side).wait_send()
 
             def one(o, _):
                 x_copy(0, o).wait_send()
@@ -273,13 +281,11 @@
             return rcopy(axS.at[o], axR.at[o], ax_ss.at[o], ax_rs.at[o], xn)
 
         def az(d, t):
-            rows = pl.ds(64 * d, 64) if t == 0 else slice(None)
+            rows = opposite(d) if t == 0 else slice(None)
             return rcopy(azS.at[d, t, rows], azR.at[d, t, rows], az_ss.at[d, t], az_rs.at[d, t], to[d])
 
-        def bz(d, t):
-            if t == 0:
-                return rcopy(bzS.at[d, 0, d], bzR.at[d, 0, d], bz_ss.at[d, 0], bz_rs.at[d, 0], to[d])
-            return rcopy(bzS.at[d, t], bzR.at[d, t], bz_ss.at[d, t], bz_rs.at[d, t], to[d])
+        def bz(d, t, j):
+            return rcopy(bzS.at[d, t, j], bzR.at[d, t, j], bz_ss.at[d, t, j], bz_rs.at[d, t, j], to[d])
 
         def bx():
             return rcopy(bxS, bxR, bx_ss.at[0], bx_rs.at[0], xn)
@@ -288,65 +294,68 @@
             o = order(i)
             for j in range(2):
                 prod[2 * o + j] = nn(match[...], refs[2 * o + j])
-            axS[o] = prod[2 * o + other, 0:HALF].astype(BF16)
+            axS[o] = prod[2 * o + other, 0:NA].astype(BF16)
             ax(o).start()
 
         multiply(0)
         for d in range(2):
-            bzS[d, 0, d] = prod[2 * toward(d, 0) + d, HALF:Q].astype(BF16)
-            bz(d, 0).start()
+            bzS[d, 0, d] = prod[2 * toward(d, 0) + d, NA:Q].astype(BF16)
+            bz(d, 0, d).start()
         multiply(1)
         multiply(2)
         idle(0)
         o = toward(0, 0)
         ax(o).wait_recv()
         for d in range(2):
-            rows = slice(64 * d, 64 * d + 64)
+            rows = opposite(d)
             azS[d, 0, rows] = (prod[2 * o + xl, rows] + axR[o, rows].astype(F32)).astype(BF16)
             az(d, 0).start()
         for t in range(1, 4):
-            for d in range(2):
-                o = toward(d, t)
-                bz(d, t - 1).wait_recv()
-                for j in range(2):
-                    s = prod[2 * o + j, HALF:Q]
+            for j in range(2):
+                for d in range(2):
+                    s = prod[2 * toward(d, t) + j, NA:Q]
                     if t > 1 or j == d:
+                        bz(d, t - 1, j).wait_recv()
                         s = s + bzR[d, t - 1, j].astype(F32)
                     bzS[d, t, j] = s.astype(BF16)
-                bz(d, t).start()
+                    bz(d, t, j).start()
             for i in range(2 * t + 1, min(2 * t + 3, Z)):
                 multiply(i)
             for d in range(2):
                 o = toward(d, t)
                 ax(o).wait_recv()
                 az(d, t - 1).wait_recv()
-                s = prod[2 * o + xl, 0:HALF] + axR[o].astype(F32)
+                s = prod[2 * o + xl, 0:NA] + axR[o].astype(F32)
                 if t > 1:
                     azS[d, t] = (s + azR[d, t - 1].astype(F32)).astype(BF16)
                 else:
                     azS[d, t] = s.astype(BF16)
-                    rows = slice(64 * d, 64 * d + 64)
-                    azS[d, t, rows] = (s[rows] + azR[d, 0, rows].astype(F32)).astype(BF16)
+                    rows = opposite(d)
+                    azS[d, t, rows] = (s[rows.start:rows.start + rows.size] + azR[d, 0, rows].astype(F32)).astype(BF16)
                 az(d, t).start()
             idle(t)
         for d in range(2):
-            bz(d, 3).wait_recv()
-        bxS[...] = (prod[2 * z + other, HALF:Q] + bzR[0, 3, other].astype(F32)
+            for j in range(2):
+                bz(d, 3, j).wait_recv()
+        bxS[...] = (prod[2 * z + other, NA:Q] + bzR[0, 3, other].astype(F32)
                     + bzR[1, 3, other].astype(F32)).astype(BF16)
         bx().start()
         ax(z).wait_recv()
         for d in range(2):
             az(d, 3).wait_recv()
-        top = (prod[own, 0:HALF] + axR[z].astype(F32) + azR[0, 3].astype(F32) + azR[1, 3].astype(F32))
-        bottom = prod[own, HALF:Q] + bzR[0, 3, xl].astype(F32) + bzR[1, 3, xl].astype(F32)
+        top = (prod[own, 0:NA] + axR[z].astype(F32) + azR[0, 3].astype(F32) + azR[1, 3].astype(F32))
+        bottom = prod[own, NA:Q] + bzR[0, 3, xl].astype(F32) + bzR[1, 3, xl].astype(F32)
         bx().wait_recv()
         bottom = bottom + bxR[...].astype(F32)
 
         def finish():
             for d in range(2):
+                bz(d, 0, d).wait_send()
                 for t in range(4):
                     az(d, t).wait_send()
-                    bz(d, t).wait_send()
+                for t in range(1, 4):
+                    for j in range(2):
+                        bz(d, t, j).wait_send()
             bx().wait_send()
 
             def one(o, _):
@@ -381,24 +390,20 @@
         return rcopy(ref, ref, ssem, rsem, target)
 
     def gax(o, x_at):
-        return same(noisy.at[2 * o + x_at, 0:HALF], gax_ss.at[o], gax_rs.at[o], xn)
+        return same(noisy.at[2 * o + x_at, 0:NA], gax_ss.at[o], gax_rs.at[o], xn)
 
     def gbx(x_at):
-        return same(noisy.at[2 * z + x_at, HALF:Q], gbx_ss.at[0], gbx_rs.at[0], xn)
+        return same(noisy.at[2 * z + x_at, NA:Q], gbx_ss.at[0], gbx_rs.at[0], xn)
 
     def gaz(d, s, o):
         if s == 4:
-            view = noisy.at[2 * o + xl, pl.ds(64 * d, 64)]
+            view = noisy.at[2 * o + xl, opposite(d)]
         else:
-            view = noisy.at[2 * o + xl, 0:HALF]
+            view = noisy.at[2 * o + xl, 0:NA]
         return same(view, gaz_ss.at[d, s - 1], gaz_rs.at[d, s - 1], to[d])
 
-    def gbz(d, s, o):
-        if s == 4:
-            view = noisy.at[2 * o + d, HALF:Q]
-        else:
-            view = noisy.at[pl.ds(2 * o, 2), HALF:Q]
-        return same(view, gbz_ss.at[d, s - 1], gbz_rs.at[d, s - 1], to[d])
+    def gbz(d, s, o, j):
+        return same(noisy.at[2 * o + j, NA:Q], gbz_ss.at[d, s - 1, j], gbz_rs.at[d, s - 1, j], to[d])
 
     def came(d, s):
         return (z + Z + (1 - 2 * d) * s) % Z
@@ -410,10 +415,12 @@
     gbx(xl).start()
     for d in range(2):
         gaz(d, 1, z).start()
+    for d in range(2):
+        gbz(d, 1, z, xl).start()
     gax(z, xl).start()
     gbx(other).wait_recv()
     for d in range(2):
-        gbz(d, 1, z).start()
+        gbz(d, 1, z, other).start()
 
     for s in range(1, 4):
         for d in range(2):
@@ -421,10 +428,12 @@
             gaz(d, s, o).wait_recv()
             gaz(d, s + 1, o).start()
             gax(o, xl).start()
-        for d in range(2):
-            o = came(d, s)
-            gbz(d, s, o).wait_recv()
-            gbz(d, s + 1, o).start()
+        for j in (xl, other) if s < 3 else (0, 1):
+            for d in range(2):
+                o = came(d, s)
+                gbz(d, s, o, j).wait_recv()
+                if s < 3 or j == d:
+                    gbz(d, s + 1, o, j).start()
         if s == 1:
             gax(z, other).wait_recv()
             score(z, True)
@@ -442,7 +451,7 @@
         gax(came(d, 3), other).wait_recv()
         score(came(d, 3))
     for d in range(2):
-        gbz(d, 4, o).wait_recv()
+        gbz(d, 4, o, d).wait_recv()
     gax(o, other).wait_recv()
     score(o)
 
@@ -457,7 +466,9 @@
         for d in range(2):
             for s in range(1, 5):
                 gaz(d, s, z).wait_send()
-                gbz(d, s, z).wait_send()
+                for j in range(2):
+                    if s < 4 or j == d:
+                        gbz(d, s, z, j).wait_send()
 
     sent.append(gather_sent)
 
@@ -540,8 +551,8 @@
             fit_ref[...] += nn(w_outT_ref[...], hidden_ref[...])
 
     top, bottom = reduce_scatter(forward)
-    shareS[0:HALF] = top
-    shareS[HALF:Q] = bottom
+    shareS[0:NA] = top
+    shareS[NA:Q] = bottom
     hear(1)
     total = jnp.sum(statR[1], axis=0)
 
@@ -755,22 +766,22 @@
             vm((2, 4, Q, W), BF16),
             vm((1, Q), jnp.int32),
             vm((Q, PAIR), BF16),
-            vm((Z, HALF, W), BF16),
-            vm((Z, HALF, W), BF16),
-            vm((2, 4, HALF, W), BF16),
-            vm((2, 4, HALF, W), BF16),
-            vm((2, 4, 2, HALF, W), BF16),
-            vm((2, 4, 2, HALF, W), BF16),
-            vm((HALF, W), BF16),
-            vm((HALF, W), BF16),
+            vm((Z, NA, W), BF16),
+            vm((Z, NA, W), BF16),
+            vm((2, 4, NA, W), BF16),
+            vm((2, 4, NA, W), BF16),
+            vm((2, 4, 2, NB, W), BF16),
+            vm((2, 4, 2, NB, W), BF16),
+            vm((NB, W), BF16),
+            vm((NB, W), BF16),
             vm((Q, W), F32),
             dma((2 * Z + 3,)), dma((2 * Z,)), dma((2 * Z,)), dma((2,)),
             dma((2, CHIPS)), dma((2, CHIPS)),
-            dma((2, Z)), dma((2, Z)), dma((2, 4)), dma((2, 4)), dma((2,)),
+            dma((2, Z)), dma((2, Z)), dma((2, 4, 2)), dma((2, 4, 2)), dma((2,)),
             dma((Z,)), dma((Z,)), dma((2, 4)), dma((2, 4)),
-            dma((2, 4)), dma((2, 4)), dma((1,)), dma((1,)),
+            dma((2, 4, 2)), dma((2, 4, 2)), dma((1,)), dma((1,)),
             dma((Z,)), dma((Z,)), dma((2, 4)), dma((2, 4)),
-            dma((2, 4)), dma((2, 4)), dma((1,)), dma((1,)),
+            dma((2, 4, 2)), dma((2, 4, 2)), dma((1,)), dma((1,)),
             dma((2,)), dma((2,)), dma((PLANE,)), dma((PLANE,)), dma((Z,)), dma((Z,)),
             dma((Z,)), dma((Z,)), dma((4,)), dma((4,)), dma((4,)), dma((4,)),
             dma((PLANE,)), dma((PLANE,)), dma((Z,)), dma((Z,)), dma((PLANE + Z,)), dma((PLANE + Z,)),

time: 150 us -> 142 us (0.947)
  Pallas kernels: 149 us -> 141 us
    pallas_call x1, Pallas kernels: 147 us -> 139 us  [main_call(): pl.pallas_call(main_kernel, out_shape=[jax.ShapeDtypeStruct((PDIM, HID),...]
where the time goes in v5:
time: 142 us
  Pallas kernels  141 us (99%)
    pallas_call x1, Pallas kernels, main_call(): pl.pallas_call(main_kernel, out_shape=[jax.ShapeDtypeStruct((PDIM, HID),...  139 us

profile of v5, /device:TPU:1, one launch (start us, length us, event | category | flops | bytes accessed | tf_op | source)
XLA Modules:
  0.0 141.5 jit_solution(2878167723259947156)
XLA Ops:
  0.6 138.6 %denoise_step.1 = (f32[192,768]{1,0:T(8,128)}, f32[192,768]{1,0:T(8,128)}, f32[8,768]{1,0:T(8,128)}) custom-call(bf16[256,12288]{1,0:T(8,128)(2,1)} %noise_hbm.1, bf16[288,12288]{1,0:T(8,128)(2,1)} %refs_hbm.1, s32[1,256]{1,0:T(1,128)} %bitcast.6, s32[1,256]{1,0:T(1,128)} %bitcast.7, bf16[192,768]{1,0:T(8,128)(2,1)} %w_in_hbm.1, f32[768]{0:T(1024)} %bias_ref.1, ...), custom_call_target="tpu_custom_call" | custom-call | tf_op jit(solution)/shard_map/denoise_step/pallas_call | solution.py:725
  139.2 2.3 %write_results.1 = (f32[192,768]{1,0:T(8,128)}, f32[192,768]{1,0:T(8,128)}, f32[768]{0:T(1024)}, f32[768]{0:T(1024)}, f32[1,1]{1,0:T(1,128)}) custom-call(f32[192,768]{1,0:T(8,128)} %get-tuple-element.13.g_in_ref, f32[192,768]{1,0:T(8,128)} %get-tuple-element.14.g_outT_ref, f32[8,768]{1,0:T(8,128)} %get-tuple-element.15.small_ref), custom_call_target="tpu_custom_call" | custom-call | tf_op jit(solution)/shard_map/write_results/pallas_call | solution.py:806

commit v6 on v5

--- a/solution.py
+++ b/solution.py
@@ -280,9 +280,9 @@
         def ax(o):
             return rcopy(axS.at[o], axR.at[o], ax_ss.at[o], ax_rs.at[o], xn)
 
-        def az(d, t):
-            rows = opposite(d) if t == 0 else slice(None)
-            return rcopy(azS.at[d, t, rows], azR.at[d, t, rows], az_ss.at[d, t], az_rs.at[d, t], to[d])
+        def az(d, t, h):
+            rows = opposite(h)
+            return rcopy(azS.at[d, t, rows], azR.at[d, t, rows], az_ss.at[d, t, h], az_rs.at[d, t, h], to[d])
 
         def bz(d, t, j):
             return rcopy(bzS.at[d, t, j], bzR.at[d, t, j], bz_ss.at[d, t, j], bz_rs.at[d, t, j], to[d])
@@ -309,7 +309,7 @@
         for d in range(2):
             rows = opposite(d)
             azS[d, 0, rows] = (prod[2 * o + xl, rows] + axR[o, rows].astype(F32)).astype(BF16)
-            az(d, 0).start()
+            az(d, 0, d).start()
         for t in range(1, 4):
             for j in range(2):
                 for d in range(2):
@@ -322,17 +322,17 @@
             for i in range(2 * t + 1, min(2 * t + 3, Z)):
                 multiply(i)
             for d in range(2):
-                o = toward(d, t)
-                ax(o).wait_recv()
-                az(d, t - 1).wait_recv()
-                s = prod[2 * o + xl, 0:NA] + axR[o].astype(F32)
-                if t > 1:
-                    azS[d, t] = (s + azR[d, t - 1].astype(F32)).astype(BF16)
-                else:
-                    azS[d, t] = s.astype(BF16)
-                    rows = opposite(d)
-                    azS[d, t, rows] = (s[rows.start:rows.start + rows.size] + azR[d, 0, rows].astype(F32)).astype(BF16)
-                az(d, t).start()
+                ax(toward(d, t)).wait_recv()
+            for h in range(2):
+                for d in range(2):
+                    o = toward(d, t)
+                    rows = opposite(h)
+                    s = prod[2 * o + xl, rows] + axR[o, rows].astype(F32)
+                    if t > 1 or h == d:
+                        az(d, t - 1, h).wait_recv()
+                        s = s + azR[d, t - 1, rows].astype(F32)
+                    azS[d, t, rows] = s.astype(BF16)
+                    az(d, t, h).start()
             idle(t)
         for d in range(2):
             for j in range(2):
@@ -342,7 +342,8 @@
         bx().start()
         ax(z).wait_recv()
         for d in range(2):
-            az(d, 3).wait_recv()
+            for h in range(2):
+                az(d, 3, h).wait_recv()
         top = (prod[own, 0:NA] + axR[z].astype(F32) + azR[0, 3].astype(F32) + azR[1, 3].astype(F32))
         bottom = prod[own, NA:Q] + bzR[0, 3, xl].astype(F32) + bzR[1, 3, xl].astype(F32)
         bx().wait_recv()
@@ -350,11 +351,11 @@
 
         def finish():
             for d in range(2):
+                az(d, 0, d).wait_send()
                 bz(d, 0, d).wait_send()
-                for t in range(4):
-                    az(d, t).wait_send()
                 for t in range(1, 4):
                     for j in range(2):
+                        az(d, t, j).wait_send()
                         bz(d, t, j).wait_send()
             bx().wait_send()
 
@@ -395,12 +396,8 @@
     def gbx(x_at):
         return same(noisy.at[2 * z + x_at, NA:Q], gbx_ss.at[0], gbx_rs.at[0], xn)
 
-    def gaz(d, s, o):
-        if s == 4:
-            view = noisy.at[2 * o + xl, opposite(d)]
-        else:
-            view = noisy.at[2 * o + xl, 0:NA]
-        return same(view, gaz_ss.at[d, s - 1], gaz_rs.at[d, s - 1], to[d])
+    def gaz(d, s, o, h):
+        return same(noisy.at[2 * o + xl, opposite(h)], gaz_ss.at[d, s - 1, h], gaz_rs.at[d, s - 1, h], to[d])
 
     def gbz(d, s, o, j):
         return same(noisy.at[2 * o + j, NA:Q], gbz_ss.at[d, s - 1, j], gbz_rs.at[d, s - 1, j], to[d])
@@ -413,8 +410,9 @@
         dots[...] = part if first else dots[...] + part
 
     gbx(xl).start()
-    for d in range(2):
-        gaz(d, 1, z).start()
+    for h in range(2):
+        for d in range(2):
+            gaz(d, 1, z, h).start()
     for d in range(2):
         gbz(d, 1, z, xl).start()
     gax(z, xl).start()
@@ -423,11 +421,14 @@
         gbz(d, 1, z, other).start()
 
     for s in range(1, 4):
+        for h in range(2):
+            for d in range(2):
+                o = came(d, s)
+                gaz(d, s, o, h).wait_recv()
+                if s < 3 or h == d:
+                    gaz(d, s + 1, o, h).start()
         for d in range(2):
-            o = came(d, s)
-            gaz(d, s, o).wait_recv()
-            gaz(d, s + 1, o).start()
-            gax(o, xl).start()
+            gax(came(d, s), xl).start()
         for j in (xl, other) if s < 3 else (0, 1):
             for d in range(2):
                 o = came(d, s)
@@ -445,7 +446,7 @@
     ref_sq = nt(jnp.ones((8, 128), F32), sqacc[...], precision=lax.Precision.HIGHEST)[0:1]
     o = came(0, 4)
     for d in range(2):
-        gaz(d, 4, o).wait_recv()
+        gaz(d, 4, o, d).wait_recv()
     gax(o, xl).start()
     for d in range(2):
         gax(came(d, 3), other).wait_recv()
@@ -465,57 +466,12 @@
         lax.fori_loop(0, Z, one, 0)
         for d in range(2):
             for s in range(1, 5):
-                gaz(d, s, z).wait_send()
                 for j in range(2):
                     if s < 4 or j == d:
+                        gaz(d, s, z, j).wait_send()
                         gbz(d, s, z, j).wait_send()
 
     sent.append(gather_sent)
-
-    halfS[...] = 2.0 * dots[...] - ref_sq
-    half = rcopy(halfS, halfR, half_sem.at[0], half_sem.at[1], sib)
-    half.start()
-    sent.append(half.wait_send)
-    half.wait_recv()
-    logits = (halfS[...] + halfR[...]) / (2.0 * sigma_col * sigma_col)
-    dots[...] = logits
-
-    def stat(i, k):
-        peer = ((chip + k) % CHIPS) * 2 + core
-        return rcopy(statS.at[i], statR.at[i, k], stat_ss.at[i, k], stat_rs.at[i, k], peer)
-
-    def tell(i, col):
-        statS[i] = row_of(col)[0:1]
-        statR[i, 0] = statS[i]
-
-        def one(k, _):
-            stat(i, k).start()
-            return 0
-
-        lax.fori_loop(1, CHIPS, one, 0)
-
-        def told():
-            def one(k, _):
-                stat(i, k).wait_send()
-                return 0
-
-            lax.fori_loop(1, CHIPS, one, 0)
-
-        sent.append(told)
-
-    def hear(i):
-        def one(k, _):
-            stat(i, k).wait_recv()
-            return 0
-
-        lax.fori_loop(1, CHIPS, one, 0)
-
-    mine = jnp.max(logits, axis=1, keepdims=True)
-    tell(0, mine)
-    dots[...] = jnp.exp(logits - mine)
-    hear(0)
-    peak = column(jnp.max(statR[0], axis=0))
-    match[...] = (dots[...] * jnp.exp(mine - peak)).astype(BF16)
 
     def patches(t):
         return jnp.concatenate([t[0:PDIM], t[PDIM:W]], axis=1)
@@ -533,22 +489,71 @@
     def forward(t):
         if t == 0:
             tell(1, jnp.sum(match[...].astype(F32), axis=1, keepdims=True))
+        elif t == 1:
+            fit_ref[...] += nn(w_outT_ref[...], hidden_ref[...])
+
+    def before(t):
+        if t == 0:
             w_in_copy.wait()
             w_out_copy.wait()
-        elif t == 1:
             x_full = patches(noisy[own].astype(F32).T)
             scaled = (c_in * x_full).astype(BF16)
             scaled_ref[...] = scaled
             fit_ref[...] = c_skip * x_full / c_out
             slope_ref[...] = (tn(w_in_ref[...], scaled) + column(w_noise_ref[...].reshape(1, HID)) * c_noise
                               + column(bias_ref[...].reshape(1, HID)))
-        elif t == 2:
+        else:
             pre = slope_ref[...]
             sig_p = jax.nn.sigmoid(pre)
             hidden_ref[...] = (pre * sig_p).astype(BF16)
             slope_ref[...] = sig_p * (1.0 + pre * (1.0 - sig_p))
-        else:
-            fit_ref[...] += nn(w_outT_ref[...], hidden_ref[...])
+
+    halfS[...] = 2.0 * dots[...] - ref_sq
+    half = rcopy(halfS, halfR, half_sem.at[0], half_sem.at[1], sib)
+    half.start()
+    sent.append(half.wait_send)
+    before(0)
+    half.wait_recv()
+    logits = (halfS[...] + halfR[...]) / (2.0 * sigma_col * sigma_col)
+    dots[...] = logits
+
+    def stat(i, k):
+        peer = ((chip + k) % CHIPS) * 2 + core
+        return rcopy(statS.at[i], statR.at[i, k], stat_ss.at[i, k], stat_rs.at[i, k], peer)
+
+    def tell(i, col):
+        statS[i] = row_of(col)[0:1]
+        statR[i, 0] = statS[i]
+
+        def one(k, _):
+            stat(i, k).start()
+            return 0
+
+        lax.fori_loop(1, CHIPS, one, 0)
+
+        def told():
+            def one(k, _):
+                stat(i, k).wait_send()
+                return 0
+
+            lax.fori_loop(1, CHIPS, one, 0)
+
+        sent.append(told)
+
+    def hear(i):
+        def one(k, _):
+            stat(i, k).wait_recv()
+            return 0
+
+        lax.fori_loop(1, CHIPS, one, 0)
+
+    mine = jnp.max(logits, axis=1, keepdims=True)
+    tell(0, mine)
+    dots[...] = jnp.exp(logits - mine)
+    before(1)
+    hear(0)
+    peak = column(jnp.max(statR[0], axis=0))
+    match[...] = (dots[...] * jnp.exp(mine - peak)).astype(BF16)
 
     top, bottom = reduce_scatter(forward)
     shareS[0:NA] = top
@@ -778,9 +783,9 @@
             dma((2 * Z + 3,)), dma((2 * Z,)), dma((2 * Z,)), dma((2,)),
             dma((2, CHIPS)), dma((2, CHIPS)),
             dma((2, Z)), dma((2, Z)), dma((2, 4, 2)), dma((2, 4, 2)), dma((2,)),
-            dma((Z,)), dma((Z,)), dma((2, 4)), dma((2, 4)),
+            dma((Z,)), dma((Z,)), dma((2, 4, 2)), dma((2, 4, 2)),
             dma((2, 4, 2)), dma((2, 4, 2)), dma((1,)), dma((1,)),
-            dma((Z,)), dma((Z,)), dma((2, 4)), dma((2, 4)),
+            dma((Z,)), dma((Z,)), dma((2, 4, 2)), dma((2, 4, 2)),
             dma((2, 4, 2)), dma((2, 4, 2)), dma((1,)), dma((1,)),
             dma((2,)), dma((2,)), dma((PLANE,)), dma((PLANE,)), dma((Z,)), dma((Z,)),
             dma((Z,)), dma((Z,)), dma((4,)), dma((4,)), dma((4,)), dma((4,)),

time: 142 us -> 140 us (0.986)
  Pallas kernels: 141 us -> 139 us
    pallas_call x1, Pallas kernels: 139 us -> 137 us  [main_call(): pl.pallas_call(main_kernel, out_shape=[jax.ShapeDtypeStruct((PDIM, HID),...]
where the time goes in v6:
time: 140 us
  Pallas kernels  139 us (99%)
    pallas_call x1, Pallas kernels, main_call(): pl.pallas_call(main_kernel, out_shape=[jax.ShapeDtypeStruct((PDIM, HID),...  137 us

profile of v6, /device:TPU:1, one launch (start us, length us, event | category | flops | bytes accessed | tf_op | source)
XLA Modules:
  0.0 140.1 jit_solution(16074702559375088820)
XLA Ops:
  0.6 137.1 %denoise_step.1 = (f32[192,768]{1,0:T(8,128)}, f32[192,768]{1,0:T(8,128)}, f32[8,768]{1,0:T(8,128)}) custom-call(bf16[256,12288]{1,0:T(8,128)(2,1)} %noise_hbm.1, bf16[288,12288]{1,0:T(8,128)(2,1)} %refs_hbm.1, s32[1,256]{1,0:T(1,128)} %bitcast.6, s32[1,256]{1,0:T(1,128)} %bitcast.7, bf16[192,768]{1,0:T(8,128)(2,1)} %w_in_hbm.1, f32[768]{0:T(1024)} %bias_ref.1, ...), custom_call_target="tpu_custom_call" | custom-call | tf_op jit(solution)/shard_map/denoise_step/pallas_call | solution.py:730
  137.8 2.3 %write_results.1 = (f32[192,768]{1,0:T(8,128)}, f32[192,768]{1,0:T(8,128)}, f32[768]{0:T(1024)}, f32[768]{0:T(1024)}, f32[1,1]{1,0:T(1,128)}) custom-call(f32[192,768]{1,0:T(8,128)} %get-tuple-element.13.g_in_ref, f32[192,768]{1,0:T(8,128)} %get-tuple-element.14.g_outT_ref, f32[8,768]{1,0:T(8,128)} %get-tuple-element.15.small_ref), custom_call_target="tpu_custom_call" | custom-call | tf_op jit(solution)/shard_map/write_results/pallas_call | solution.py:811
